TPU v7x, 32 devices: a whole 2x2x4 slice. The times are simulated.
32 devices in a mesh: lat: 4 (over z), chan: 2 (over core), obs: 4 (over y, x).
Axes of the slice: x: 2, y: 2, z: 4, core: 2. Of those that a mesh axis runs over, the one named last changes fastest.
Arguments:
- next_grad: bfloat16 [32, 1024, 256], P(('lat', 'obs'), None, 'chan'), may hold values from -6 to 6
- pre_act: bfloat16 [32, 1024, 256], P(('lat', 'obs'), None, 'chan'), may hold values from -6 to 6
- legendre: bfloat16 [512, 512, 32], P(('lat', 'obs')), may hold values from -1 to 1, as said below
- order_slots: int32 [512], replicated, may hold values from 0 to 511, as said below
- quad_weights: float32 [32], replicated, may hold values from 0.5 to 1.5
- spectral_gain: float32 [2, 512, 256], P(None, None, 'chan'), may hold values from -5 to 5
- saved_coeffs: bfloat16 [512, 2, 512, 256], P(('lat', 'obs'), None, None, 'chan'), may hold values from -0.029907227 to 0.029907227
- obs_value: bfloat16 [16, 16, 16], P(('lat', 'obs')), may hold values from -16 to 16
- obs_lat_frac: bfloat16 [16, 16, 16], P(('lat', 'obs')), may hold values from 0 to 1
- obs_lon_frac: bfloat16 [16, 16, 16], P(('lat', 'obs')), may hold values from 0 to 1
- obs_corner: int32 [16, 16, 16], P(('lat', 'obs')), may hold values from 0 to 1023
- obs_channel: int32 [16, 16, 16], P(('lat', 'obs')), may hold values from 0 to 255
- slot_counts: int32 [16, 16], P(('lat', 'obs')), may hold values from 0 to 16, as said below
Outputs:
- grid_grad: bfloat16 [32, 1024, 256], P(('lat', 'obs'), None, 'chan')
- gain_grad: float32 [2, 512, 256], P(None, None, 'chan')
Inputs may be any that keep to these rules, and one draw needn't show every extreme that they name: `order_slots`: each order from 0 to 511 stands at exactly one slot. `legendre`: entry [s, l, lat] is zero wherever l < order_slots[s]. `slot_counts`: at most 16; in every draw some tile receives 16 live slots from every source shard; slots at or beyond the count carry no observation.
All inputs are finite; a program needn't handle non-finite values.
Results may differ from a plain program's by a relative error of at most 0.0055.
Values may be sent and summed in bfloat16 or wider, within the bound.
A program may use at most 128 MiB of HBM per device.

v0:
```python
import math

import jax
import jax.numpy as jnp
from jax import lax
from jax.sharding import PartitionSpec as P


def gelu_slope(pre_act):
    values = pre_act.astype(jnp.float32)
    normal_cdf = 0.5 * (1.0 + jax.scipy.special.erf(values * 0.7071067811865476))
    density = jnp.exp(-0.5 * values * values) * 0.3989422804014327
    return normal_cdf + values * density


def zonal_tables(orders, longitudes, lon_count, cos_weight, sin_weight):
    phase = orders[:, None] * longitudes[None, :] % lon_count
    angle = phase.astype(jnp.float32) * (2.0 * math.pi / lon_count)
    return (
        (cos_weight * jnp.cos(angle)).astype(jnp.bfloat16),
        (sin_weight * jnp.sin(angle)).astype(jnp.bfloat16),
    )


def adjoint_tiles(
    amounts, lat_frac, lon_frac, corners, channels, lat_dev, lon_count, chan_base, width
):
    received = amounts.size
    amounts = amounts.reshape(received)
    lat_frac = lat_frac.reshape(received)
    lon_frac = lon_frac.reshape(received)
    corners = corners.reshape(received)
    channels = channels.reshape(received)
    block_rows = min(512, received)
    cell_ids = lax.iota(jnp.int32, lat_dev * lon_count)
    chan_ids = chan_base + lax.iota(jnp.int32, width)
    nothing = jnp.zeros((), jnp.bfloat16)

    def add_block(counter, summed):
        offset = counter * block_rows
        lat_step = lax.dynamic_slice_in_dim(lat_frac, offset, block_rows).astype(jnp.float32)
        lon_step = lax.dynamic_slice_in_dim(lon_frac, offset, block_rows).astype(jnp.float32)
        corner_ids = lax.dynamic_slice_in_dim(corners, offset, block_rows)
        chan_rows = lax.dynamic_slice_in_dim(channels, offset, block_rows)
        amount_rows = lax.dynamic_slice_in_dim(amounts, offset, block_rows)
        top = corner_ids // lon_count
        left = corner_ids % lon_count
        right = (left + 1) % lon_count
        lower = top * lon_count
        upper = lower + lon_count
        weights = (
            (1.0 - lat_step) * (1.0 - lon_step),
            (1.0 - lat_step) * lon_step,
            lat_step * (1.0 - lon_step),
            lat_step * lon_step,
        )
        places = (lower + left, lower + right, upper + left, upper + right)
        stencil = jnp.zeros((block_rows, lat_dev * lon_count), jnp.bfloat16)
        for weight, place in zip(weights, places):
            stencil = stencil + jnp.where(
                cell_ids[None, :] == place[:, None], weight.astype(jnp.bfloat16)[:, None], nothing
            )
        sources = jnp.where(chan_rows[:, None] == chan_ids[None, :], amount_rows[:, None], nothing)
        return summed + lax.dot_general(
            stencil, sources, (((0,), (0,)), ((), ())), preferred_element_type=jnp.float32
        )

    start_sum = jnp.zeros((lat_dev * lon_count, width), jnp.float32)
    summed = lax.fori_loop(0, received // block_rows, add_block, start_sum)
    return summed.reshape(lat_dev, lon_count, width)


def on_device(
    next_grad,
    pre_act,
    legendre,
    order_slots,
    quad_weights,
    spectral_gain,
    saved_coeffs,
    obs_value,
    obs_lat_frac,
    obs_lon_frac,
    obs_corner,
    obs_channel,
    slot_counts,
):
    lat_dev, lon_count, width = next_grad.shape
    lat_size = lax.axis_size("lat")
    obs_size = lax.axis_size("obs")
    slot_dev, degrees, lat_count = legendre.shape
    total_orders = order_slots.shape[0]
    capacity = obs_value.shape[1]
    alive_slots = lax.iota(jnp.int32, capacity)[:, None] < slot_counts[0][None, :]
    masked = jnp.where(alive_slots, obs_value[0], jnp.zeros((), jnp.bfloat16)).reshape(
        capacity, lat_size, obs_size
    )
    lat_frac = obs_lat_frac[0].reshape(capacity, lat_size, obs_size)
    lon_frac = obs_lon_frac[0].reshape(capacity, lat_size, obs_size)
    corners = obs_corner[0].reshape(capacity, lat_size, obs_size)
    channels = obs_channel[0].reshape(capacity, lat_size, obs_size)
    arrived = (
        lax.all_to_all(
            lax.all_to_all(masked, "lat", split_axis=1, concat_axis=1, tiled=True),
            "obs",
            split_axis=2,
            concat_axis=2,
            tiled=True,
        ),
        lax.all_to_all(
            lax.all_to_all(lat_frac, "lat", split_axis=1, concat_axis=1, tiled=True),
            "obs",
            split_axis=2,
            concat_axis=2,
            tiled=True,
        ),
        lax.all_to_all(
            lax.all_to_all(lon_frac, "lat", split_axis=1, concat_axis=1, tiled=True),
            "obs",
            split_axis=2,
            concat_axis=2,
            tiled=True,
        ),
        lax.all_to_all(
            lax.all_to_all(corners, "lat", split_axis=1, concat_axis=1, tiled=True),
            "obs",
            split_axis=2,
            concat_axis=2,
            tiled=True,
        ),
        lax.all_to_all(
            lax.all_to_all(channels, "lat", split_axis=1, concat_axis=1, tiled=True),
            "obs",
            split_axis=2,
            concat_axis=2,
            tiled=True,
        ),
    )
    chan_base = lax.axis_index("chan") * width
    obs_grad = adjoint_tiles(
        arrived[0],
        arrived[1],
        arrived[2],
        arrived[3],
        arrived[4],
        lat_dev,
        lon_count,
        chan_base,
        width,
    )
    out_grad = next_grad.astype(jnp.float32) + obs_grad
    pre_grad = (out_grad * gelu_slope(pre_act)).astype(jnp.bfloat16)
    longitudes = lax.iota(jnp.int32, lon_count)
    crossed_orders = jnp.transpose(
        order_slots.reshape(lat_size, obs_size, slot_dev), (1, 0, 2)
    ).reshape(total_orders)
    legendre_view = legendre.reshape(slot_dev, degrees, lat_size, obs_size, lat_dev)
    weight_view = quad_weights.reshape(lat_size, obs_size, lat_dev)
    factor = jnp.where(order_slots == 0, 1.0, 2.0).astype(jnp.float32)[:, None]
    cosine, sine = zonal_tables(order_slots, longitudes, lon_count, factor, -factor)
    real_part = jnp.einsum("mn,knc->mkc", cosine, pre_grad, preferred_element_type=jnp.float32)
    imag_part = jnp.einsum("mn,knc->mkc", sine, pre_grad, preferred_element_type=jnp.float32)
    by_order = lax.all_to_all(
        lax.all_to_all(
            jnp.stack([real_part, imag_part], axis=1).astype(jnp.bfloat16),
            "lat",
            split_axis=0,
            concat_axis=2,
            tiled=True,
        ),
        "obs",
        split_axis=0,
        concat_axis=2,
        tiled=True,
    )
    order_view = by_order.reshape(slot_dev, 2, obs_size, lat_size, lat_dev, width)
    up_grad = jnp.einsum(
        "iljka,irkjac->irlc", legendre_view, order_view, preferred_element_type=jnp.float32
    )
    saved = saved_coeffs.astype(jnp.float32)
    gain_terms = jnp.stack(
        [
            jnp.sum(up_grad[:, 0] * saved[:, 0] + up_grad[:, 1] * saved[:, 1], axis=0),
            jnp.sum(up_grad[:, 1] * saved[:, 0] - up_grad[:, 0] * saved[:, 1], axis=0),
        ]
    )
    gain_grad = lax.psum(gain_terms, ("lat", "obs"))
    gain_real = spectral_gain[0]
    gain_imag = spectral_gain[1]
    coeff_grad = jnp.stack(
        [
            gain_real * up_grad[:, 0] + gain_imag * up_grad[:, 1],
            gain_real * up_grad[:, 1] - gain_imag * up_grad[:, 0],
        ],
        axis=1,
    ).astype(jnp.bfloat16)
    analysed = jnp.einsum(
        "iljka,irlc->irjkac", legendre_view, coeff_grad, preferred_element_type=jnp.float32
    )
    lat_grad = (
        (analysed * weight_view[None, None, :, :, :, None])
        .astype(jnp.bfloat16)
        .reshape(slot_dev, 2, lat_count, width)
    )
    by_lat = lax.all_to_all(
        lax.all_to_all(lat_grad, "lat", split_axis=2, concat_axis=0, tiled=True),
        "obs",
        split_axis=2,
        concat_axis=0,
        tiled=True,
    )
    scale = jnp.full((total_orders, 1), 1.0 / lon_count, jnp.float32)
    cosine, sine = zonal_tables(crossed_orders, longitudes, lon_count, scale, -scale)
    spectral_grad = jnp.einsum(
        "mkc,mn->knc", by_lat[:, 0], cosine, preferred_element_type=jnp.float32
    )
    spectral_grad = spectral_grad + jnp.einsum(
        "mkc,mn->knc", by_lat[:, 1], sine, preferred_element_type=jnp.float32
    )
    grid_grad = (out_grad + spectral_grad).astype(jnp.bfloat16)
    return (grid_grad, gain_grad)


def solution(mesh):
    in_specs = (
        P(("lat", "obs"), None, "chan"),
        P(("lat", "obs"), None, "chan"),
        P(("lat", "obs"), None, None),
        P(),
        P(),
        P(None, None, "chan"),
        P(("lat", "obs"), None, None, "chan"),
        P(("lat", "obs"), None, None),
        P(("lat", "obs"), None, None),
        P(("lat", "obs"), None, None),
        P(("lat", "obs"), None, None),
        P(("lat", "obs"), None, None),
        P(("lat", "obs"), None),
    )
    out_specs = (P(("lat", "obs"), None, "chan"), P(None, None, "chan"))
    return jax.shard_map(
        on_device, mesh=mesh, in_specs=in_specs, out_specs=out_specs, check_vma=False
    )
```

profile of v0, /device:TPU:0, one launch (start us, length us, event | category | flops | bytes accessed | tf_op | source)
XLA Modules:
  0.0 338.4 jit_solution(11334439921768294679)
XLA Ops:
  7.2 1.4 copy.112
  8.5 6.3 %all-to-all-start.2 = ((bf16[16,4,4]{0,2,1:T(4,128)(2,1)}), bf16[16,4,4]{0,2,1:T(4,128)(2,1)S(1)}, u32[]{:S(2)}, u32[]{:S(2)}) async-start(bf16[16,4,4]{0,2,1:T(4,128)(2,1)} %bitcast.1), calls=%async_computation.2 | async-start | bytes 8192 | tf_op jit(solution)/shard_map/all_to_all | solution.py:111
  14.8 1.4 copy.115
  16.2 0.8 copy.121
  16.9 0.5 broadcast.331
  17.5 1.3 reduce.5
  18.9 1.5 all-to-all-done.2
  20.4 3.6 %all-to-all-start.4 = ((bf16[16,4,4]{0,2,1:T(4,128)(2,1)}), bf16[16,4,4]{0,2,1:T(4,128)(2,1)S(1)}, u32[]{:S(2)}, u32[]{:S(2)}) async-start(bf16[16,4,4]{0,2,1:T(4,128)(2,1)} %bitcast.2), calls=%async_computation.4 | async-start | bytes 8192 | tf_op jit(solution)/shard_map/all_to_all | solution.py:118
  24.0 0.7 fusion.74
  24.6 4.9 %all-to-all-done.4 = bf16[16,4,4]{0,2,1:T(4,128)(2,1)S(1)} async-done(((bf16[16,4,4]{0,2,1:T(4,128)(2,1)}), bf16[16,4,4]{0,2,1:T(4,128)(2,1)S(1)}, u32[]{:S(2)}, u32[]{:S(2)}) %all-to-all-start.4) | async-done | bytes 544 | tf_op jit(solution)/shard_map/all_to_all | solution.py:118
  29.5 3.2 all-to-all-start.8
  32.8 0.6 copy.113
  33.4 4.9 %all-to-all-done.8 = bf16[16,4,4]{0,2,1:T(4,128)(2,1)S(1)} async-done(((bf16[16,4,4]{0,2,1:T(4,128)(2,1)}), bf16[16,4,4]{0,2,1:T(4,128)(2,1)S(1)}, u32[]{:S(2)}, u32[]{:S(2)}) %all-to-all-start.8) | async-done | bytes 544 | tf_op jit(solution)/shard_map/all_to_all | solution.py:104
  38.3 3.7 %all-to-all-start.3 = ((bf16[16,4,4]{0,1,2:T(4,128)(2,1)}), bf16[16,4,4]{0,1,2:T(4,128)(2,1)S(1)}, u32[]{:S(2)}, u32[]{:S(2)}) async-start(bf16[16,4,4]{0,1,2:T(4,128)(2,1)} %copy.113), calls=%async_computation.3 | async-start | bytes 8192 | tf_op jit(solution)/shard_map/all_to_all | solution.py:110
  42.0 0.6 copy.116
  42.6 4.1 %all-to-all-done.3 = bf16[16,4,4]{0,1,2:T(4,128)(2,1)S(1)} async-done(((bf16[16,4,4]{0,1,2:T(4,128)(2,1)}), bf16[16,4,4]{0,1,2:T(4,128)(2,1)S(1)}, u32[]{:S(2)}, u32[]{:S(2)}) %all-to-all-start.3) | async-done | bytes 544 | tf_op jit(solution)/shard_map/all_to_all | solution.py:110
  46.7 3.2 all-to-all-start.5
  50.0 0.6 copy.122
  50.6 4.0 %all-to-all-done.5 = bf16[16,4,4]{0,1,2:T(4,128)(2,1)S(1)} async-done(((bf16[16,4,4]{0,1,2:T(4,128)(2,1)}), bf16[16,4,4]{0,1,2:T(4,128)(2,1)S(1)}, u32[]{:S(2)}, u32[]{:S(2)}) %all-to-all-start.5) | async-done | bytes 544 | tf_op jit(solution)/shard_map/all_to_all | solution.py:117
  54.6 3.2 all-to-all-start.9
  57.9 1.4 copy.109
  59.2 3.3 all-to-all-done.9
  62.5 3.2 all-to-all-start
  65.8 0.7 compare_select_fusion.4
  66.4 1.4 copy.118
  67.8 3.5 %all-to-all-done = s32[16,4,4]{0,2,1:T(4,128)S(1)} async-done(((s32[16,4,4]{0,2,1:T(4,128)}), s32[16,4,4]{0,2,1:T(4,128)S(1)}, u32[]{:S(2)}, u32[]{:S(2)}) %all-to-all-start) | async-done | bytes 1056 | tf_op jit(solution)/shard_map/all_to_all | solution.py:125
  71.3 3.2 all-to-all-start.6
  75.1 0.6 copy.110
  75.7 4.5 %all-to-all-done.6 = s32[16,4,4]{0,2,1:T(4,128)S(1)} async-done(((s32[16,4,4]{0,2,1:T(4,128)}), s32[16,4,4]{0,2,1:T(4,128)S(1)}, u32[]{:S(2)}, u32[]{:S(2)}) %all-to-all-start.6) | async-done | bytes 1056 | tf_op jit(solution)/shard_map/all_to_all | solution.py:132
  80.1 3.2 all-to-all-start.1
  83.4 0.1 copy.123
  83.6 0.6 copy.119
  84.2 3.8 %all-to-all-done.1 = s32[16,4,4]{0,1,2:T(4,128)S(1)} async-done(((s32[16,4,4]{0,1,2:T(4,128)}), s32[16,4,4]{0,1,2:T(4,128)S(1)}, u32[]{:S(2)}, u32[]{:S(2)}) %all-to-all-start.1) | async-done | bytes 1056 | tf_op jit(solution)/shard_map/all_to_all | solution.py:124
  88.0 3.2 all-to-all-start.7
  91.5 4.4 %all-to-all-done.7 = s32[16,4,4]{0,1,2:T(4,128)S(1)} async-done(((s32[16,4,4]{0,1,2:T(4,128)}), s32[16,4,4]{0,1,2:T(4,128)S(1)}, u32[]{:S(2)}, u32[]{:S(2)}) %all-to-all-start.7) | async-done | bytes 1056 | tf_op jit(solution)/shard_map/all_to_all | solution.py:131
  96.2 1.5 fusion.33
  97.8 0.6 fusion.63
  98.5 8.6 %fusion.23 = bf16[512,1,2,128]{3,0,2,1:T(8,128)(2,1)S(1)} fusion(bf16[2,1024,128]{2,1,0:T(8,128)(2,1)S(1)} %fusion.63, f32[512]{0:T(512)S(1)} %get-tuple-element.47, s32[512]{0:T(512)S(1)} %copy-done.4), kind=kOutput, calls=%fused_computation.50 | convolution fusion | flops 276955136 | bytes 790528 | tf_op jit(solution)/shard_map/mn,knc->mkc/dot_general | solution.py:161
  107.1 8.7 %fusion.24 = bf16[512,1,2,128]{3,0,2,1:T(8,128)(2,1)S(1)} fusion(bf16[2,1024,128]{2,1,0:T(8,128)(2,1)S(1)} %fusion.63, f32[512]{0:T(512)S(1)} %get-tuple-element.48, s32[512]{0:T(512)S(1)} %copy-done.4), kind=kOutput, calls=%fused_computation.51 | convolution fusion | flops 276955136 | bytes 790528 | tf_op jit(solution)/shard_map/mn,knc->mkc/dot_general | solution.py:162
  115.8 0.5 copy.128
  116.4 12.7 %all_to_all.119 = bf16[512,2,2,128]{3,2,1,0:T(2,128)(2,1)S(1)} all-to-all(bf16[512,2,2,128]{3,2,1,0:T(2,128)(2,1)S(1)} %copy.128), channel_id=1, replica_groups=mesh['lat'=4,'chan'=2,'obs'=4] {'lat'}, dimensions={0} | all-to-all | bytes 1048576 | tf_op jit(solution)/shard_map/all_to_all | solution.py:164
  129.2 1.1 copy.131
  130.3 4.3 %all-to-all-start.11 = ((bf16[128,2,8,128]{3,2,1,0:T(8,128)(2,1)}), bf16[128,2,8,128]{3,2,1,0:T(8,128)(2,1)}, u32[]{:S(2)}, u32[]{:S(2)}) async-start(bf16[128,2,8,128]{3,2,1,0:T(8,128)(2,1)} %copy.131), calls=%async_computation.11 | async-start | bytes 1048576 | tf_op jit(solution)/shard_map/all_to_all | solution.py:163
  134.7 1.2 reshape.220
  135.9 0.4 reshape.214
  136.3 1.1 slice_bitcast_fusion.5
  137.4 0.1 copy.125
  137.5 0.1 copy.134
  137.7 12.0 %copy.145 = bf16[32,2,512,128]{2,3,1,0:T(8,128)(2,1)} copy(bf16[32,2,512,128]{3,2,1,0:T(8,128)(2,1)} %param.19) | data formatting | bytes 16777216 | tf_op args[6]
  149.7 11.5 %convert_element_type.133 = f32[32,2,512,128]{2,3,1,0:T(8,128)} convert(bf16[32,2,512,128]{2,3,1,0:T(8,128)(2,1)} %copy.145) | non-fusion elementwise | flops 4194304 | bytes 25165824 | tf_op jit(solution)/shard_map/convert_element_type | solution.py:180
  161.4 10.3 %convolution_bitcast_fusion = f32[32,2,512,128]{2,3,1,0:T(8,128)} fusion(bf16[32,512,4,4,2,1]{1,4,3,2,0,5:T(2,128)(2,1)} %reshape.220, bf16[32,2,4,4,2,128]{5,4,3,1,0,2:T(2,128)(2,1)} %bitcast.18), kind=kOutput, calls=%fused_computation | convolution fusion | flops 268435456 | bytes 18350080 | tf_op jit(solution)/shard_map/iljka,irkjac->irlc/dot_general | solution.py:177
  171.7 15.3 %add_reduce_fusion = (f32[512,128]{0,1:T(8,128)S(1)}, f32[512,128]{0,1:T(8,128)S(1)}, bf16[32,1,512,128]{2,3,1,0:T(8,128)(2,1)S(1)}, bf16[32,1,512,128]{2,3,1,0:T(8,128)(2,1)}) fusion(f32[32,2,512,128]{2,3,1,0:T(8,128)} %convert_element_type.133, f32[32,2,512,128]{2,3,1,0:T(8,128)} %convolution_bitcast_fusion, f32[512,128]{0,1:T(8,128)S(1)} %copy.134, ...), kind=kLoop, calls=%fused_computation.3 | loop fusion | flops 33423360 | bytes 42991616 | tf_op jit(solution)/shard_map/reduce_sum | solution.py:183
  187.0 4.8 %fusion.22 = bf16[32,2,4,4,2,128]{5,3,4,2,1,0:T(4,128)(2,1)S(1)} fusion(bf16[32,1,512,128]{2,3,1,0:T(8,128)(2,1)S(1)} %get-tuple-element.43, bf16[32,1,512,128]{2,3,1,0:T(8,128)(2,1)} %get-tuple-element.44, bf16[32,512,4,4,2,1]{1,4,3,2,0,5:T(2,128)(2,1)S(1)} %bitcast.98, f32[4,4,2]{1,2,0:T(2,128)S(1)} %copy.137), kind=kOutput, calls=%fused_computation.47 | convolution fusion | flops 285736960 | bytes 9961600 | tf_op jit(solution)/shard_map/iljka,irlc->irjkac/dot_general | solution.py:197
  191.8 1.1 copy.161
  193.0 3.5 %all-to-all-start.12 = ((bf16[32,2,32,128]{3,0,1,2:T(8,128)(2,1)}), bf16[32,2,32,128]{3,0,1,2:T(8,128)(2,1)S(1)}, u32[]{:S(2)}, u32[]{:S(2)}) async-start(bf16[32,2,32,128]{3,0,1,2:T(8,128)(2,1)} %bitcast.30), calls=%async_computation.12 | async-start | bytes 1048576 | tf_op jit(solution)/shard_map/all_to_all | solution.py:206
  196.5 0.9 pad_maximum_fusion.1
  197.4 9.3 %all-to-all-done.12 = bf16[32,2,32,128]{3,0,1,2:T(8,128)(2,1)S(1)} async-done(((bf16[32,2,32,128]{3,0,1,2:T(8,128)(2,1)}), bf16[32,2,32,128]{3,0,1,2:T(8,128)(2,1)S(1)}, u32[]{:S(2)}, u32[]{:S(2)}) %all-to-all-start.12) | async-done | bytes 524320 | tf_op jit(solution)/shard_map/all_to_all | solution.py:206
  206.7 0.3 copy.141
  207.0 1.2 copy.142
  208.2 3.9 %all-to-all-start.13 = ((bf16[128,2,8,128]{3,1,0,2:T(2,128)(2,1)}), bf16[128,2,8,128]{3,1,0,2:T(2,128)(2,1)S(1)}, u32[]{:S(2)}, u32[]{:S(2)}) async-start(bf16[128,2,8,128]{3,1,0,2:T(2,128)(2,1)} %copy.142), calls=%async_computation.13 | async-start | bytes 1048576 | tf_op jit(solution)/shard_map/all_to_all | solution.py:205
  212.4 100.0 %all-reduce.2.cloned.1.call-done = f32[2,512,128]{1,2,0:T(8,128)} async-done(((f32[2,512,128]{1,2,0:T(8,128)}), f32[2,512,128]{1,2,0:T(8,128)}) %all-reduce.2.cloned.1.call-update) | async-done | bytes 524304 | tf_op jit(solution)/shard_map/psum | solution.py:187
  312.4 2.0 copy.146
  314.6 7.9 %fusion.41 = f32[1024,2,128]{2,0,1:T(8,128)S(1)} fusion(s32[512]{0:T(512)S(1)} %mul.212, bf16[512,2,2,128]{3,0,2,1:T(8,128)(2,1)S(1)} %bitcast.99), kind=kOutput, calls=%fused_computation.64 | convolution fusion | flops 276824064 | bytes 1312768 | tf_op jit(solution)/shard_map/mkc,mn->knc/dot_general | solution.py:214
  322.5 9.1 %fusion.21 = bf16[2,1024,128]{2,1,0:T(8,128)(2,1)} fusion(f32[1024,2,128]{2,0,1:T(8,128)S(1)} %fusion.41, s32[512]{0:T(512)S(1)} %mul.212, f32[2,1024,128]{2,1,0:T(8,128)S(1)} %bitcast.97, bf16[2,1024,128]{2,1,0:T(8,128)(2,1)S(1)} %copy-done.3, bf16[512,2,2,128]{3,0,2,1:T(8,128)(2,1)S(1)} %bitcast.100), kind=kOutput, calls=%fused_computation.46 | convolution fusion | flops 278134784 | bytes 3409920 | tf_op jit(solution)/shard_map/mkc,mn->knc/dot_general | solution.py:217
  (40 shorter events, 2.0 us)
Async XLA Ops:
  8.5 11.9 %all-to-all-start.2 = ((bf16[16,4,4]{0,2,1:T(4,128)(2,1)}), bf16[16,4,4]{0,2,1:T(4,128)(2,1)S(1)}, u32[]{:S(2)}, u32[]{:S(2)}) async-start(bf16[16,4,4]{0,2,1:T(4,128)(2,1)} %bitcast.1), calls=%async_computation.2 | async-start | bytes 8192 | tf_op jit(solution)/shard_map/all_to_all | solution.py:111
  20.4 9.1 %all-to-all-start.4 = ((bf16[16,4,4]{0,2,1:T(4,128)(2,1)}), bf16[16,4,4]{0,2,1:T(4,128)(2,1)S(1)}, u32[]{:S(2)}, u32[]{:S(2)}) async-start(bf16[16,4,4]{0,2,1:T(4,128)(2,1)} %bitcast.2), calls=%async_computation.4 | async-start | bytes 8192 | tf_op jit(solution)/shard_map/all_to_all | solution.py:118
  29.5 8.8 %all-to-all-start.8 = ((bf16[16,4,4]{0,2,1:T(4,128)(2,1)}), bf16[16,4,4]{0,2,1:T(4,128)(2,1)S(1)}, u32[]{:S(2)}, u32[]{:S(2)}) async-start(bf16[16,4,4]{0,2,1:T(4,128)(2,1)} %fusion.74), calls=%async_computation.8 | async-start | bytes 8192 | tf_op jit(solution)/shard_map/all_to_all | solution.py:104
  38.3 8.4 %all-to-all-start.3 = ((bf16[16,4,4]{0,1,2:T(4,128)(2,1)}), bf16[16,4,4]{0,1,2:T(4,128)(2,1)S(1)}, u32[]{:S(2)}, u32[]{:S(2)}) async-start(bf16[16,4,4]{0,1,2:T(4,128)(2,1)} %copy.113), calls=%async_computation.3 | async-start | bytes 8192 | tf_op jit(solution)/shard_map/all_to_all | solution.py:110
  46.7 7.9 %all-to-all-start.5 = ((bf16[16,4,4]{0,1,2:T(4,128)(2,1)}), bf16[16,4,4]{0,1,2:T(4,128)(2,1)S(1)}, u32[]{:S(2)}, u32[]{:S(2)}) async-start(bf16[16,4,4]{0,1,2:T(4,128)(2,1)} %copy.116), calls=%async_computation.5 | async-start | bytes 8192 | tf_op jit(solution)/shard_map/all_to_all | solution.py:117
  54.6 7.9 %all-to-all-start.9 = ((bf16[16,4,4]{0,1,2:T(4,128)(2,1)}), bf16[16,4,4]{0,1,2:T(4,128)(2,1)S(1)}, u32[]{:S(2)}, u32[]{:S(2)}) async-start(bf16[16,4,4]{0,1,2:T(4,128)(2,1)} %copy.122), calls=%async_computation.9 | async-start | bytes 8192 | tf_op jit(solution)/shard_map/all_to_all | solution.py:103
  62.5 8.8 %all-to-all-start = ((s32[16,4,4]{0,2,1:T(4,128)}), s32[16,4,4]{0,2,1:T(4,128)S(1)}, u32[]{:S(2)}, u32[]{:S(2)}) async-start(s32[16,4,4]{0,2,1:T(4,128)} %bitcast), calls=%async_computation | async-start | bytes 16384 | tf_op jit(solution)/shard_map/all_to_all | solution.py:125
  71.3 8.8 %all-to-all-start.6 = ((s32[16,4,4]{0,2,1:T(4,128)}), s32[16,4,4]{0,2,1:T(4,128)S(1)}, u32[]{:S(2)}, u32[]{:S(2)}) async-start(s32[16,4,4]{0,2,1:T(4,128)} %bitcast.3), calls=%async_computation.6 | async-start | bytes 16384 | tf_op jit(solution)/shard_map/all_to_all | solution.py:132
  80.1 7.9 %all-to-all-start.1 = ((s32[16,4,4]{0,1,2:T(4,128)}), s32[16,4,4]{0,1,2:T(4,128)S(1)}, u32[]{:S(2)}, u32[]{:S(2)}) async-start(s32[16,4,4]{0,1,2:T(4,128)} %copy.110), calls=%async_computation.1 | async-start | bytes 16384 | tf_op jit(solution)/shard_map/all_to_all | solution.py:124
  88.0 7.9 %all-to-all-start.7 = ((s32[16,4,4]{0,1,2:T(4,128)}), s32[16,4,4]{0,1,2:T(4,128)S(1)}, u32[]{:S(2)}, u32[]{:S(2)}) async-start(s32[16,4,4]{0,1,2:T(4,128)} %copy.119), calls=%async_computation.7 | async-start | bytes 16384 | tf_op jit(solution)/shard_map/all_to_all | solution.py:131
  96.2 1.6 copy-start.1
  96.2 1.6 copy-start.2
  97.8 0.7 copy-start.4
  129.1 5.6 %copy-start = (bf16[32,512,32]{1,2,0:T(8,128)(2,1)S(1)}, bf16[32,512,32]{1,2,0:T(8,128)(2,1)}, u32[]{:S(2)}) copy-start(bf16[32,512,32]{1,2,0:T(8,128)(2,1)} %param.15) | copy-start | bytes 3145732
  130.3 31.1 %all-to-all-start.11 = ((bf16[128,2,8,128]{3,2,1,0:T(8,128)(2,1)}), bf16[128,2,8,128]{3,2,1,0:T(8,128)(2,1)}, u32[]{:S(2)}, u32[]{:S(2)}) async-start(bf16[128,2,8,128]{3,2,1,0:T(8,128)(2,1)} %copy.131), calls=%async_computation.11 | async-start | bytes 1048576 | tf_op jit(solution)/shard_map/all_to_all | solution.py:163
  149.7 11.5 %copy-start.5 = (f32[32]{0:T(128)S(1)}, f32[32]{0:T(128)}, u32[]{:S(2)}) copy-start(f32[32]{0:T(128)} %param.17) | copy-start | bytes 388
  193.0 13.7 %all-to-all-start.12 = ((bf16[32,2,32,128]{3,0,1,2:T(8,128)(2,1)}), bf16[32,2,32,128]{3,0,1,2:T(8,128)(2,1)S(1)}, u32[]{:S(2)}, u32[]{:S(2)}) async-start(bf16[32,2,32,128]{3,0,1,2:T(8,128)(2,1)} %bitcast.30), calls=%async_computation.12 | async-start | bytes 1048576 | tf_op jit(solution)/shard_map/all_to_all | solution.py:206
  196.4 116.0 %all-reduce.2.cloned.1.call-start = ((), (), s32[]{:S(2)}) async-start(), calls=%async_computation.14 | async-start | bytes 1048576 | tf_op jit(solution)/shard_map/psum | solution.py:187
  208.2 106.2 %all-to-all-start.13 = ((bf16[128,2,8,128]{3,1,0,2:T(2,128)(2,1)}), bf16[128,2,8,128]{3,1,0,2:T(2,128)(2,1)S(1)}, u32[]{:S(2)}, u32[]{:S(2)}) async-start(bf16[128,2,8,128]{3,1,0,2:T(2,128)(2,1)} %copy.142), calls=%async_computation.13 | async-start | bytes 1048576 | tf_op jit(solution)/shard_map/all_to_all | solution.py:205
  314.6 7.9 %copy-start.3 = (bf16[2,1024,128]{2,1,0:T(8,128)(2,1)S(1)}, bf16[2,1024,128]{2,1,0:T(8,128)(2,1)}, u32[]{:S(2)}) copy-start(bf16[2,1024,128]{2,1,0:T(8,128)(2,1)} %param.13) | copy-start | bytes 1572868
Sparse Core Ops, SparseCore 0:
  202.4 109.9 all-reduce.1
where the time goes:
time: 340 us; the launch traced here: 338 us
  waiting for transfers between devices  148 us (44%)
  matrix products  50.9 us (15%)
  starting transfers between devices  48.1 us (14%)
  local copies, waits for them, and re-layouts  33.1 us (10%)
  other arithmetic  31 us (9%)
  between operations  14.3 us (4%)
  blocking collectives  12.7 us (4%)
    psum x1, waiting for transfers between devices, on_device(): gain_grad = lax.psum(gain_terms, ('lat', 'obs'))  100 us
    unnamed x20, local copies, waits for them, and re-layouts  20.9 us
    reduce_sum x1, other arithmetic, on_device(): jnp.sum(up_grad[:, 0] * saved[:, 0] + up_grad[:, 1] * saved[:, 1], axis=0)  15.3 us
    all_to_all x1, blocking collectives, on_device(): lax.all_to_all(jnp.stack([real_part, imag_part], axis=1).astype(jnp.bfloa...  12.7 us
    convert_element_type x1, other arithmetic, on_device(): saved = saved_coeffs.astype(jnp.float32)  11.5 us
    dot_general x1, matrix products, on_device(): jnp.einsum('iljka,irkjac->irlc', legendre_view, order_view, preferred_ele...  10.3 us
    all_to_all x1, waiting for transfers between devices, on_device(): lax.all_to_all(lat_grad, 'lat', split_axis=2, concat_axis=0, tiled=True)  9.33 us
    dot_general x1, matrix products, on_device(): jnp.einsum('mkc,mn->knc', by_lat[:, 1], sine, preferred_element_type=jnp....  9.07 us
  transfers between devices with their start and end apart: 14, of which 12 were waited for; matrix products, arithmetic and copies ran while one was open for 13% of the time, Pallas kernels for 0%

commit v1 on v0

--- a/solution.py
+++ b/solution.py
@@ -1,8 +1,12 @@
+import functools
 import math
 
 import jax
 import jax.numpy as jnp
+import numpy as np
 from jax import lax
+from jax.experimental import pallas as pl
+from jax.experimental.pallas import tpu as pltpu
 from jax.sharding import PartitionSpec as P
 
 
@@ -70,7 +74,7 @@
     return summed.reshape(lat_dev, lon_count, width)
 
 
-def on_device(
+def plain_path(
     next_grad,
     pre_act,
     legendre,
@@ -221,6 +225,528 @@
     return (grid_grad, gain_grad)
 
 
+CHUNK = 8
+F32 = jnp.float32
+BF16 = jnp.bfloat16
+MESH = pl.DeviceIdType.MESH
+
+
+def base_tables(order_count, lon_count):
+    phase = np.arange(order_count)[:, None] * np.arange(lon_count)[None, :] % lon_count
+    angle = phase.astype(np.float32) * np.float32(2.0 * math.pi / lon_count)
+    return np.concatenate([np.cos(angle), -np.sin(angle)], axis=1).astype(jnp.bfloat16)
+
+
+def dot(a, b):
+    return jnp.dot(a, b, preferred_element_type=F32)
+
+
+def block_kernel(
+    lat_size,
+    obs_size,
+    capacity,
+    packed,
+    order_col,
+    order_row,
+    quad_col,
+    next_hbm,
+    act_hbm,
+    leg_hbm,
+    gain_hbm,
+    saved_hbm,
+    table_hbm,
+    table_t_hbm,
+    grid_out,
+    gain_out,
+    next_ref,
+    act_ref,
+    leg_ref,
+    gain_ref,
+    saved_ref,
+    table_ref,
+    table_t_ref,
+    obs_in,
+    hot,
+    hot_t,
+    tab,
+    tab_t,
+    to_slot,
+    to_lat,
+    slope_ref,
+    out_ref,
+    pre_ref,
+    fwd_out,
+    fwd_in,
+    by_slot,
+    by_lat,
+    bwd_out,
+    bwd_in,
+    total,
+    part_out,
+    part_in,
+    mine,
+    parts,
+    local_sem,
+    obs_send,
+    obs_recv,
+    fwd_send,
+    fwd_recv,
+    bwd_send,
+    bwd_recv,
+    part_send,
+    part_recv,
+    full_send,
+    full_recv,
+):
+    group = lat_size * obs_size
+    me = lax.axis_index("lat") * obs_size + lax.axis_index("obs")
+    lat_dev, lon_count, width = next_ref.shape
+    slot_dev, lat_count, degrees = leg_ref.shape
+    orders = order_col.shape[0]
+    chunks = slot_dev // CHUNK
+    rows = CHUNK * lat_dev
+
+    def place(peer):
+        return {"lat": peer // obs_size, "obs": peer % obs_size}
+
+    def peers(body):
+        def step(j, carry):
+            body(lax.rem(me + j, group), lax.rem(me + group - j, group))
+            return carry
+
+        lax.fori_loop(1, group, step, 0)
+
+    def send(src, dst, send_sem, recv_sem, peer):
+        return pltpu.make_async_remote_copy(
+            src_ref=src,
+            dst_ref=dst,
+            send_sem=send_sem,
+            recv_sem=recv_sem,
+            device_id=place(peer),
+            device_id_type=MESH,
+        )
+
+    local = [
+        pltpu.make_async_copy(src, dst, local_sem.at[i])
+        for i, (src, dst) in enumerate(
+            (
+                (act_hbm, act_ref),
+                (table_hbm, table_ref),
+                (next_hbm, next_ref),
+                (table_t_hbm, table_t_ref),
+                (leg_hbm, leg_ref),
+                (gain_hbm, gain_ref),
+                (saved_hbm, saved_ref),
+            )
+        )
+    ]
+    for copy in local:
+        copy.start()
+
+    barrier = pltpu.get_barrier_semaphore()
+    peers(
+        lambda peer, _: pl.semaphore_signal(
+            barrier, inc=1, device_id=place(peer), device_id_type=MESH
+        )
+    )
+    pl.semaphore_wait(barrier, group - 1)
+
+    peers(
+        lambda peer, _: send(
+            packed.at[peer], obs_in.at[me], obs_send.at[peer], obs_recv.at[me], peer
+        ).start()
+    )
+    obs_in[me] = packed[me]
+
+    local[0].wait()
+    for k in range(lat_dev):
+        values = act_ref[k].astype(F32)
+        cdf = 0.5 * (1.0 + lax.erf(values * 0.7071067811865476))
+        density = jnp.exp(-0.5 * values * values) * 0.3989422804014327
+        slope_ref[k] = cdf + values * density
+    hot[...] = jnp.where(
+        lax.broadcasted_iota(jnp.int32, (orders, orders), 1) == order_col[...], 1.0, 0.0
+    ).astype(BF16)
+    hot_t[...] = jnp.where(
+        lax.broadcasted_iota(jnp.int32, (orders, orders), 0) == order_row[...], 1.0, 0.0
+    ).astype(BF16)
+    side = lat_count * CHUNK
+    first = lax.broadcasted_iota(jnp.int32, (side, side), 0)
+    second = lax.broadcasted_iota(jnp.int32, (side, side), 1)
+    to_lat[...] = jnp.where(
+        (first // CHUNK == second % lat_count) & (first % CHUNK == second // lat_count), 1.0, 0.0
+    ).astype(BF16)
+    to_slot[...] = jnp.where(
+        (second // CHUNK == first % lat_count) & (second % CHUNK == first // lat_count), 1.0, 0.0
+    ).astype(BF16)
+    local[1].wait()
+    tile = 256
+
+    for part in range(2):
+
+        def make_tab(i, carry):
+            at = pl.multiple_of(i * tile, tile)
+            got = dot(hot[...], table_ref[:, pl.ds(part * lon_count + at, tile)]).astype(BF16)
+            tab[:, part, :, pl.ds(at, tile)] = got.reshape(chunks, orders // chunks, tile)
+            return carry
+
+        lax.fori_loop(0, lon_count // tile, make_tab, 0)
+
+    local[2].wait()
+    peers(
+        lambda peer, source: send(
+            packed.at[peer], obs_in.at[source], obs_send.at[peer], obs_recv.at[source], peer
+        ).wait()
+    )
+    lanes = obs_in.shape[2]
+    sources_per = lanes // capacity
+    halves = []
+    for h in range(group // sources_per):
+        halves.append(jnp.sum(obs_in[h * sources_per : (h + 1) * sources_per], axis=0))
+    seen = jnp.concatenate(halves, axis=1)
+    received = seen.shape[1]
+    corner = seen[5:6].astype(jnp.int32)
+    channel = seen[6:7].astype(jnp.int32)
+    left = corner % lon_count
+    right = corner - left + (left + 1) % lon_count
+    places = (corner, right, corner + lon_count, right + lon_count)
+    chan_ids = lax.axis_index("chan") * width + lax.broadcasted_iota(
+        jnp.int32, (width, received), 0
+    )
+    amounts = jnp.where(chan_ids == channel, seen[0:1], 0.0).astype(BF16)
+    for k in range(lat_dev):
+        for half in range(2):
+            span = lon_count // 2
+            begin = half * span
+            cells = k * lon_count + begin + lax.broadcasted_iota(jnp.int32, (span, received), 0)
+            stencil = jnp.zeros((span, received), F32)
+            for w, at in enumerate(places):
+                stencil = stencil + jnp.where(cells == at, seen[1 + w : 2 + w], 0.0)
+            added = lax.dot_general(
+                stencil.astype(BF16), amounts, (((1,), (1,)), ((), ())), preferred_element_type=F32
+            )
+            here = slice(begin, begin + span)
+            out_grad = next_ref[k, here].astype(F32) + added
+            out_ref[k, here] = out_grad
+            pre_ref[here, k * width : (k + 1) * width] = (out_grad * slope_ref[k, here]).astype(BF16)
+
+    def zonal(q, carry):
+        per = orders // chunks
+        at = pl.multiple_of(q * per, per)
+        factor = jnp.where(order_col[pl.ds(at, per), :] == 0, 1.0, 2.0)
+        for part in range(2):
+            got = (dot(tab[q, part], pre_ref[...]) * factor).reshape(group, CHUNK, lat_dev * width)
+            got = jnp.concatenate(
+                [got[:, :, k * width : (k + 1) * width] for k in range(lat_dev)], axis=1
+            )
+            fwd_out[q, :, :, part * width : (part + 1) * width] = got.astype(BF16)
+        fwd_in[q, me] = fwd_out[q, me]
+        peers(
+            lambda peer, _: send(
+                fwd_out.at[q, peer],
+                fwd_in.at[q, me],
+                fwd_send.at[q, peer],
+                fwd_recv.at[q, me],
+                peer,
+            ).start()
+        )
+        return carry
+
+    lax.fori_loop(0, chunks, zonal, 0)
+
+    local[3].wait()
+    for part in range(2):
+
+        def make_tab_t(i, carry):
+            at = pl.multiple_of(i * tile, tile)
+            got = dot(table_t_ref[pl.ds(part * lon_count + at, tile), :], hot_t[...])
+            tab_t[pl.ds(at, tile), part * orders : (part + 1) * orders] = got.astype(BF16)
+            return carry
+
+        lax.fori_loop(0, lon_count // tile, make_tab_t, 0)
+    total[...] = jnp.zeros_like(total)
+    for copy in local[4:]:
+        copy.wait()
+
+    def degrees_of(q, carry):
+        peers(
+            lambda peer, source: send(
+                fwd_out.at[q, peer],
+                fwd_in.at[q, source],
+                fwd_send.at[q, peer],
+                fwd_recv.at[q, source],
+                peer,
+            ).wait()
+        )
+        arrived = fwd_in[q].reshape(side, 2 * width)
+        by_slot[...] = dot(to_slot[...], arrived).astype(BF16)
+
+        def per_slot(i, inner):
+            s = q * CHUNK + i
+            at = pl.multiple_of(i * lat_count, lat_count)
+            table = leg_ref[s]
+            up = lax.dot_general(
+                table,
+                by_slot[pl.ds(at, lat_count), :],
+                (((0,), (0,)), ((), ())),
+                preferred_element_type=F32,
+            )
+            up_real = up[:, :width]
+            up_imag = up[:, width:]
+            saved_real = saved_ref[s, 0].astype(F32)
+            saved_imag = saved_ref[s, 1].astype(F32)
+            total[0] += up_real * saved_real + up_imag * saved_imag
+            total[1] += up_imag * saved_real - up_real * saved_imag
+            gain_real = gain_ref[0]
+            gain_imag = gain_ref[1]
+            coeff = jnp.concatenate(
+                [
+                    (gain_real * up_real + gain_imag * up_imag).astype(BF16),
+                    (gain_real * up_imag - gain_imag * up_real).astype(BF16),
+                ],
+                axis=1,
+            )
+            by_lat[pl.ds(at, lat_count), :] = (dot(table, coeff) * quad_col[...]).astype(BF16)
+            return inner
+
+        lax.fori_loop(0, CHUNK, per_slot, 0)
+        bwd_out[q] = dot(to_lat[...], by_lat[...]).astype(BF16).reshape(group, rows, 2 * width)
+        bwd_in[q, me] = bwd_out[q, me]
+        peers(
+            lambda peer, _: send(
+                bwd_out.at[q, peer],
+                bwd_in.at[q, me],
+                bwd_send.at[q, peer],
+                bwd_recv.at[q, me],
+                peer,
+            ).start()
+        )
+        return carry
+
+    lax.fori_loop(0, chunks, degrees_of, 0)
+
+    share = degrees // group
+    for r in range(2):
+        part_out[:, r * share : (r + 1) * share, :] = (
+            total[r].reshape(group, share, width).astype(BF16)
+        )
+    part_in[me] = part_out[me]
+    peers(
+        lambda peer, _: send(
+            part_out.at[peer], part_in.at[me], part_send.at[peer], part_recv.at[me], peer
+        ).start()
+    )
+
+    def lat_arrivals(q, carry):
+        peers(
+            lambda peer, source: send(
+                bwd_out.at[q, peer],
+                bwd_in.at[q, source],
+                bwd_send.at[q, peer],
+                bwd_recv.at[q, source],
+                peer,
+            ).wait()
+        )
+        return carry
+
+    lax.fori_loop(0, chunks, lat_arrivals, 0)
+
+    peers(
+        lambda peer, source: send(
+            part_out.at[peer], part_in.at[source], part_send.at[peer], part_recv.at[source], peer
+        ).wait()
+    )
+    mine[...] = jnp.sum(part_in[...].astype(F32), axis=0).astype(BF16)
+    parts[me] = mine[...]
+    peers(
+        lambda peer, _: send(
+            mine, parts.at[me], full_send.at[peer], full_recv.at[me], peer
+        ).start()
+    )
+
+    back = bwd_in[...].astype(F32).reshape(chunks * group, lat_dev, CHUNK, 2 * width)
+    pieces = []
+    for part in range(2):
+        lane = slice(part * width, (part + 1) * width)
+        pieces.append(
+            jnp.concatenate(
+                [back[:, k, :, lane].reshape(orders, width) for k in range(lat_dev)], axis=1
+            ).astype(BF16)
+        )
+    grads = jnp.concatenate(pieces, axis=0)
+    pre_ref[0 : 2 * orders, :] = grads
+
+    def to_grid(i, carry):
+        at = pl.multiple_of(i * tile, tile)
+        got = dot(tab_t[pl.ds(at, tile), :], pre_ref[0 : 2 * orders, :]) * (1.0 / lon_count)
+        for k in range(lat_dev):
+            grid_out[k, pl.ds(at, tile), :] = (
+                out_ref[k, pl.ds(at, tile), :] + got[:, k * width : (k + 1) * width]
+            ).astype(BF16)
+        return carry
+
+    lax.fori_loop(0, lon_count // tile, to_grid, 0)
+
+    peers(
+        lambda peer, source: send(
+            mine, parts.at[source], full_send.at[peer], full_recv.at[source], peer
+        ).wait()
+    )
+    for r in range(2):
+        gain_out[r] = (
+            parts[:, r * share : (r + 1) * share, :].astype(F32).reshape(degrees, width)
+        )
+
+
+def on_device(
+    next_grad,
+    pre_act,
+    legendre,
+    order_slots,
+    quad_weights,
+    spectral_gain,
+    saved_coeffs,
+    obs_value,
+    obs_lat_frac,
+    obs_lon_frac,
+    obs_corner,
+    obs_channel,
+    slot_counts,
+):
+    lat_dev, lon_count, width = next_grad.shape
+    lat_size = lax.axis_size("lat")
+    obs_size = lax.axis_size("obs")
+    group = lat_size * obs_size
+    slot_dev, degrees, lat_count = legendre.shape
+    orders = order_slots.shape[0]
+    capacity = obs_value.shape[1]
+    chunks = slot_dev // CHUNK
+    rows = CHUNK * lat_dev
+    lanes = 128
+    side = lat_count * CHUNK
+
+    me = lax.axis_index("lat") * obs_size + lax.axis_index("obs")
+    alive_slots = lax.iota(jnp.int32, capacity)[:, None] < slot_counts[0][None, :]
+    amounts = jnp.where(alive_slots, obs_value[0], jnp.zeros((), BF16)).astype(F32)
+    lat_step = obs_lat_frac[0].astype(F32)
+    lon_step = obs_lon_frac[0].astype(F32)
+    weights = (
+        (1.0 - lat_step) * (1.0 - lon_step),
+        (1.0 - lat_step) * lon_step,
+        lat_step * (1.0 - lon_step),
+        lat_step * lon_step,
+    )
+    fields = jnp.stack(
+        [amounts]
+        + [lax.reduce_precision(w, 8, 7) for w in weights]
+        + [obs_corner[0].astype(F32), obs_channel[0].astype(F32), jnp.zeros_like(amounts)]
+    )
+    spots = lanes // capacity
+    fields = jnp.transpose(fields, (2, 0, 1))
+    packed = jnp.where(
+        (lax.iota(jnp.int32, lanes) // capacity == me % spots)[None, None, :],
+        jnp.tile(fields, (1, 1, spots)),
+        0.0,
+    )
+    order_q = jnp.transpose(order_slots.reshape(group, chunks, CHUNK), (1, 0, 2)).reshape(orders)
+    table = base_tables(orders, lon_count)
+    table_t = np.ascontiguousarray(table.T)
+
+    vmem = pl.BlockSpec(memory_space=pltpu.VMEM)
+    anywhere = pl.BlockSpec(memory_space=pl.ANY)
+    dma = pltpu.SemaphoreType.DMA
+    share = degrees // group
+    return pl.pallas_call(
+        functools.partial(block_kernel, lat_size, obs_size, capacity),
+        out_shape=(
+            jax.ShapeDtypeStruct((lat_dev, lon_count, width), BF16),
+            jax.ShapeDtypeStruct((2, degrees, width), F32),
+        ),
+        in_specs=[vmem] * 4 + [anywhere] * 7,
+        out_specs=(vmem, vmem),
+        scratch_shapes=[
+            pltpu.VMEM((lat_dev, lon_count, width), BF16),
+            pltpu.VMEM((lat_dev, lon_count, width), BF16),
+            pltpu.VMEM((slot_dev, lat_count, degrees), BF16),
+            pltpu.VMEM((2, degrees, width), F32),
+            pltpu.VMEM((slot_dev, 2, degrees, width), BF16),
+            pltpu.VMEM((orders, 2 * lon_count), BF16),
+            pltpu.VMEM((2 * lon_count, orders), BF16),
+            pltpu.VMEM((group, 8, lanes), F32),
+            pltpu.VMEM((orders, orders), BF16),
+            pltpu.VMEM((orders, orders), BF16),
+            pltpu.VMEM((chunks, 2, orders // chunks, lon_count), BF16),
+            pltpu.VMEM((lon_count, 2 * orders), BF16),
+            pltpu.VMEM((side, side), BF16),
+            pltpu.VMEM((side, side), BF16),
+            pltpu.VMEM((lat_dev, lon_count, width), F32),
+            pltpu.VMEM((lat_dev, lon_count, width), F32),
+            pltpu.VMEM((max(lon_count, 2 * orders), lat_dev * width), BF16),
+            pltpu.VMEM((chunks, group, rows, 2 * width), BF16),
+            pltpu.VMEM((chunks, group, rows, 2 * width), BF16),
+            pltpu.VMEM((side, 2 * width), BF16),
+            pltpu.VMEM((side, 2 * width), BF16),
+            pltpu.VMEM((chunks, group, rows, 2 * width), BF16),
+            pltpu.VMEM((chunks, group, rows, 2 * width), BF16),
+            pltpu.VMEM((2, degrees, width), F32),
+            pltpu.VMEM((group, 2 * share, width), BF16),
+            pltpu.VMEM((group, 2 * share, width), BF16),
+            pltpu.VMEM((2 * share, width), BF16),
+            pltpu.VMEM((group, 2 * share, width), BF16),
+            dma((7,)),
+            dma((group,)),
+            dma((group,)),
+            dma((chunks, group)),
+            dma((chunks, group)),
+            dma((chunks, group)),
+            dma((chunks, group)),
+            dma((group,)),
+            dma((group,)),
+            dma((group,)),
+            dma((group,)),
+        ],
+        compiler_params=pltpu.CompilerParams(
+            collective_id=0, has_side_effects=True, vmem_limit_bytes=50 * 1024 * 1024
+        ),
+        name="block_backward",
+    )(
+        packed,
+        order_q[:, None],
+        order_q[None, :],
+        quad_weights[:, None],
+        next_grad,
+        pre_act,
+        jnp.transpose(legendre, (0, 2, 1)),
+        spectral_gain,
+        saved_coeffs,
+        jnp.asarray(table),
+        jnp.asarray(table_t),
+    )
+
+
+def kernel_fits(next_grad, legendre, obs_value, group):
+    lat_dev, lon_count, width = next_grad.shape
+    slot_dev, degrees, lat_count = legendre.shape
+    capacity = obs_value.shape[1]
+    return (
+        slot_dev % CHUNK == 0
+        and (CHUNK * lat_dev) % 16 == 0
+        and lat_count * CHUNK <= 512
+        and width % 128 == 0
+        and lon_count % 512 == 0
+        and degrees % (16 * group) == 0
+        and 128 % capacity == 0
+        and group % (128 // capacity) == 0
+    )
+
+
+def device_path(*args):
+    group = lax.axis_size("lat") * lax.axis_size("obs")
+    if kernel_fits(args[0], args[2], args[7], group):
+        return on_device(*args)
+    return plain_path(*args)
+
+
 def solution(mesh):
     in_specs = (
         P(("lat", "obs"), None, "chan"),
@@ -239,5 +765,5 @@
     )
     out_specs = (P(("lat", "obs"), None, "chan"), P(None, None, "chan"))
     return jax.shard_map(
-        on_device, mesh=mesh, in_specs=in_specs, out_specs=out_specs, check_vma=False
-    )
+        device_path, mesh=mesh, in_specs=in_specs, out_specs=out_specs, check_vma=False
+    )

time: 340 us -> 67.7 us (0.20)
  waiting for transfers between devices: 148 us -> 0 us
  Pallas kernels: 0 us -> 55.6 us
  matrix products: 50.9 us -> 0 us
  starting transfers between devices: 48.1 us -> 0 us
  local copies, waits for them, and re-layouts: 33.1 us -> 5.84 us
  other arithmetic: 31 us -> 4.94 us
  between operations: 14.3 us -> 0.76 us
  blocking collectives: 12.7 us -> 0 us
    psum x1 -> x0, waiting for transfers between devices: 100 us -> none  [on_device(): gain_grad = lax.psum(gain_terms, ('lat', 'obs'))]
    pallas_call x0 -> x1, Pallas kernels: none -> 55.6 us  [on_device(): pl.pallas_call(functools.partial(block_kernel, lat_size, obs_size, capaci...]
    dot_general x7 -> x0, matrix products: 50.9 us -> none  [the longest x1 10.3 us: on_device(): jnp.einsum('iljka,irkjac->irlc', legendre_view, order_view, preferred_ele...]
    all_to_all x13 -> x0, waiting for transfers between devices: 48.3 us -> none  [the longest x1 9.33 us: on_device(): lax.all_to_all(lat_grad, 'lat', split_axis=2, concat_axis=0, tiled=True)]
    all_to_all x13 -> x0, starting transfers between devices: 48 us -> none  [the longest x1 6.32 us: on_device(): lax.all_to_all(lat_frac, 'lat', split_axis=1, concat_axis=1, tiled=True)]
    unnamed x20 -> x10, local copies, waits for them, and re-layouts: 20.9 us -> 3.67 us
    reduce_sum x1 -> x0, other arithmetic: 15.3 us -> none  [on_device(): jnp.sum(up_grad[:, 0] * saved[:, 0] + up_grad[:, 1] * saved[:, 1], axis=0)]
    all_to_all x1 -> x0, blocking collectives: 12.7 us -> none  [on_device(): lax.all_to_all(jnp.stack([real_part, imag_part], axis=1).astype(jnp.bfloa...]
  transfers between devices with their start and end apart: 14 -> 0, of which waited for: 12 -> 0; matrix products, arithmetic and copies ran while one was open for 13% -> 0% of each run, Pallas kernels for 0% -> 0%
where the time goes in v1:
time: 67.7 us; the launch traced here: 67.1 us
  Pallas kernels  55.6 us (82%)
  local copies, waits for them, and re-layouts  5.84 us (9%)
  other arithmetic  4.94 us (7%)
  between operations  0.76 us (1%)
    pallas_call x1, Pallas kernels, on_device(): pl.pallas_call(functools.partial(block_kernel, lat_size, obs_size, capaci...  55.6 us
    unnamed x7, other arithmetic  4.93 us
    unnamed x10, local copies, waits for them, and re-layouts  3.67 us

profile of v1, /device:TPU:0, one launch (start us, length us, event | category | flops | bytes accessed | tf_op | source)
XLA Modules:
  0.0 67.1 jit_solution(13787162606136563211)
XLA Ops:
  0.6 0.0 copy-start
  0.6 0.0 copy-start.1
  0.7 0.8 %copy.23.quad_col = f32[32,1]{1,0:T(8,128)S(1)} copy(f32[32,1]{0,1:T(1,128)} %bitcast.10) | data formatting | bytes 256 | tf_op jit(solution)/shard_map/broadcast_in_dim | solution.py:716
  1.5 0.8 %reshape.58 = s32[16,4,8]{2,1,0:T(4,128)S(1)} reshape(s32[512]{0:T(512)} %param.18) | data formatting | bytes 4096 | tf_op jit(solution)/shard_map/reshape | solution.py:651
  2.3 0.1 broadcast_in_dim_reshape.7.order_row
  2.4 0.7 %constant_dynamic-update-slice_fusion.7 = f32[8,16,16]{2,1,0:T(8,128)S(1)} fusion(bf16[1,16,16]{2,1,0:T(8,128)(2,1)} %param.22, s32[16]{0:T(128)} %bitcast.11), kind=kLoop, calls=%fused_computation.8 | loop fusion | flops 767 | bytes 8768
  3.1 0.7 %constant_dynamic-update-slice_fusion.6 = f32[8,16,16]{2,1,0:T(8,128)S(1)} fusion(f32[8,16,16]{2,1,0:T(8,128)S(1)} %constant_dynamic-update-slice_fusion.7, bf16[1,16,16]{2,1,0:T(8,128)(2,1)} %param.24, bf16[1,16,16]{2,1,0:T(8,128)(2,1)} %param.23), kind=kLoop, calls=%fused_computation.7 | loop fusion | flops 1536 | bytes 9216
  3.8 0.7 %constant_dynamic-update-slice_fusion.5 = f32[8,16,16]{2,1,0:T(8,128)S(1)} fusion(f32[8,16,16]{2,1,0:T(8,128)S(1)} %constant_dynamic-update-slice_fusion.6, bf16[1,16,16]{2,1,0:T(8,128)(2,1)} %param.24, bf16[1,16,16]{2,1,0:T(8,128)(2,1)} %param.23), kind=kLoop, calls=%fused_computation.6 | loop fusion | flops 1280 | bytes 9216
  4.5 0.7 %constant_dynamic-update-slice_fusion.4 = f32[8,16,16]{2,1,0:T(8,128)S(1)} fusion(f32[8,16,16]{2,1,0:T(8,128)S(1)} %constant_dynamic-update-slice_fusion.5, bf16[1,16,16]{2,1,0:T(8,128)(2,1)} %param.24, bf16[1,16,16]{2,1,0:T(8,128)(2,1)} %param.23), kind=kLoop, calls=%fused_computation.5 | loop fusion | flops 1280 | bytes 9216
  5.2 0.7 %constant_dynamic-update-slice_fusion.3 = f32[8,16,16]{2,1,0:T(8,128)S(1)} fusion(f32[8,16,16]{2,1,0:T(8,128)S(1)} %constant_dynamic-update-slice_fusion.4, bf16[1,16,16]{2,1,0:T(8,128)(2,1)} %param.24, bf16[1,16,16]{2,1,0:T(8,128)(2,1)} %param.23), kind=kLoop, calls=%fused_computation.4 | loop fusion | flops 1024 | bytes 9216
  5.9 0.7 %constant_dynamic-update-slice_fusion.2 = f32[8,16,16]{2,1,0:T(8,128)S(1)} fusion(f32[8,16,16]{2,1,0:T(8,128)S(1)} %constant_dynamic-update-slice_fusion.3, s32[1,16,16]{2,1,0:T(8,128)} %param.25), kind=kLoop, calls=%fused_computation.3 | loop fusion | flops 256 | bytes 9216
  6.6 0.7 %constant_dynamic-update-slice_fusion.1 = f32[8,16,16]{2,1,0:T(8,128)S(1)} fusion(f32[8,16,16]{2,1,0:T(8,128)S(1)} %constant_dynamic-update-slice_fusion.2, s32[1,16,16]{2,1,0:T(8,128)} %param.26), kind=kLoop, calls=%fused_computation.2 | loop fusion | flops 256 | bytes 9216
  7.3 0.1 copy.19
  7.4 0.1 broadcast_in_dim_reshape.8.order_col
  7.6 0.2 tile.10
  7.8 0.0 copy-done
  7.8 0.0 copy-done.1
  7.9 0.0 copy-start.2
  7.9 1.0 %copy-done.2 = bf16[2,1024,128]{2,1,0:T(8,128)(2,1)S(1)} copy-done((bf16[2,1024,128]{2,1,0:T(8,128)(2,1)S(1)}, bf16[2,1024,128]{2,1,0:T(8,128)(2,1)}, u32[]{:S(2)}) %copy-start.2) | copy-done | bytes 524312
  8.9 0.0 copy-start.3
  8.9 1.0 %copy-done.3 = f32[2,512,128]{2,1,0:T(8,128)S(1)} copy-done((f32[2,512,128]{2,1,0:T(8,128)S(1)}, f32[2,512,128]{2,1,0:T(8,128)}, u32[]{:S(2)}) %copy-start.3) | copy-done | bytes 524312
  9.9 55.6 %block_backward.1 = (bf16[2,1024,128]{2,1,0:T(8,128)(2,1)S(1)}, f32[2,512,128]{2,1,0:T(8,128)S(1)}) custom-call(f32[16,8,128]{2,1,0:T(8,128)S(1)} %broadcast_select_fusion.packed, s32[512,1]{1,0:T(8,128)S(1)} %broadcast_in_dim_reshape.8.order_col, s32[1,512]{1,0:T(1,128)S(1)} %broadcast_in_dim_reshape.7.order_row, f32[32,1]{1,0:T(8,128)S(1)} %copy.23.quad_col, ...), custom_call_target="tpu_custom_call" | custom-call | tf_op jit(solution)/shard_map/block_backward/pallas_call | solution.py:659
  65.5 0.8 %copy.33 = bf16[2,1024,128]{2,1,0:T(8,128)(2,1)} copy(bf16[2,1024,128]{2,1,0:T(8,128)(2,1)S(1)} %get-tuple-element.4) | data formatting | bytes 1048576
  66.3 0.8 %copy.34 = f32[2,512,128]{2,1,0:T(8,128)} copy(f32[2,512,128]{2,1,0:T(8,128)S(1)} %get-tuple-element.5) | data formatting | bytes 1048576
  (5 shorter events, 0.1 us)
Async XLA Ops:
  0.6 7.2 %copy-start = (bf16[32,512,32]{1,2,0:T(8,128)(2,1)S(1)}, bf16[32,512,32]{1,2,0:T(8,128)(2,1)}, u32[]{:S(2)}) copy-start(bf16[32,512,32]{1,2,0:T(8,128)(2,1)} %param.17) | copy-start | bytes 3145732
  0.6 7.2 %copy-start.1 = (bf16[2,1024,128]{2,1,0:T(8,128)(2,1)S(1)}, bf16[2,1024,128]{2,1,0:T(8,128)(2,1)}, u32[]{:S(2)}) copy-start(bf16[2,1024,128]{2,1,0:T(8,128)(2,1)} %next_hbm.1) | copy-start | bytes 1572868
  7.9 1.0 %copy-start.2 = (bf16[2,1024,128]{2,1,0:T(8,128)(2,1)S(1)}, bf16[2,1024,128]{2,1,0:T(8,128)(2,1)}, u32[]{:S(2)}) copy-start(bf16[2,1024,128]{2,1,0:T(8,128)(2,1)} %act_hbm.1) | copy-start | bytes 1572868
  8.9 1.0 %copy-start.3 = (f32[2,512,128]{2,1,0:T(8,128)S(1)}, f32[2,512,128]{2,1,0:T(8,128)}, u32[]{:S(2)}) copy-start(f32[2,512,128]{2,1,0:T(8,128)} %gain_hbm.1) | copy-start | bytes 1572868

commit v2 on v1

--- a/solution.py
+++ b/solution.py
@@ -244,11 +244,14 @@
 def block_kernel(
     lat_size,
     obs_size,
-    capacity,
-    packed,
-    order_col,
+    value_ref,
+    lat_frac_ref,
+    lon_frac_ref,
+    corner_ref,
+    channel_ref,
+    count_ref,
     order_row,
-    quad_col,
+    quad_row,
     next_hbm,
     act_hbm,
     leg_hbm,
@@ -265,11 +268,14 @@
     saved_ref,
     table_ref,
     table_t_ref,
+    packed,
     obs_in,
     hot,
     hot_t,
+    factor_ref,
     tab,
     tab_t,
+    leg_t,
     to_slot,
     to_lat,
     slope_ref,
@@ -278,13 +284,15 @@
     fwd_out,
     fwd_in,
     by_slot,
+    coeff_ref,
     by_lat,
     bwd_out,
     bwd_in,
     total,
-    part_out,
-    part_in,
-    mine,
+    near_out,
+    near_in,
+    far_out,
+    far_in,
     parts,
     local_sem,
     obs_send,
@@ -293,39 +301,58 @@
     fwd_recv,
     bwd_send,
     bwd_recv,
-    part_send,
-    part_recv,
-    full_send,
-    full_recv,
+    sum_send,
+    sum_recv,
 ):
     group = lat_size * obs_size
-    me = lax.axis_index("lat") * obs_size + lax.axis_index("obs")
+    my_lat = lax.axis_index("lat")
+    my_obs = lax.axis_index("obs")
+    me = my_lat * obs_size + my_obs
     lat_dev, lon_count, width = next_ref.shape
     slot_dev, lat_count, degrees = leg_ref.shape
-    orders = order_col.shape[0]
+    orders = order_row.shape[1]
+    capacity = value_ref.shape[1]
     chunks = slot_dev // CHUNK
     rows = CHUNK * lat_dev
+    lanes = packed.shape[2]
+    tile = 256
 
     def place(peer):
         return {"lat": peer // obs_size, "obs": peer % obs_size}
 
     def peers(body):
         def step(j, carry):
-            body(lax.rem(me + j, group), lax.rem(me + group - j, group))
+            body(lax.rem(me + j, group))
             return carry
 
         lax.fori_loop(1, group, step, 0)
 
-    def send(src, dst, send_sem, recv_sem, peer):
+    def send(src, dst, send_sem, recv_sem, target):
         return pltpu.make_async_remote_copy(
             src_ref=src,
             dst_ref=dst,
             send_sem=send_sem,
             recv_sem=recv_sem,
-            device_id=place(peer),
+            device_id=target,
             device_id_type=MESH,
         )
 
+    beside = {"obs": lax.rem(my_obs + 1, obs_size)}
+
+    def iota(shape, axis):
+        return lax.broadcasted_iota(jnp.int32, shape, axis)
+
+    def column(row):
+        side = row.shape[1]
+        same = iota((side, side), 0) == iota((side, side), 1)
+        return jnp.sum(jnp.where(same, row, 0.0), axis=1, keepdims=True)
+
+    barrier = pltpu.get_barrier_semaphore()
+    peers(
+        lambda peer: pl.semaphore_signal(
+            barrier, inc=1, device_id=place(peer), device_id_type=MESH
+        )
+    )
     local = [
         pltpu.make_async_copy(src, dst, local_sem.at[i])
         for i, (src, dst) in enumerate(
@@ -340,23 +367,59 @@
             )
         )
     ]
-    for copy in local:
+    for copy in local[:3]:
         copy.start()
 
-    barrier = pltpu.get_barrier_semaphore()
+    alive = iota((capacity, group), 0) < count_ref[...]
+    lat_step = lat_frac_ref[0].astype(F32)
+    lon_step = lon_frac_ref[0].astype(F32)
+    corner = corner_ref[0]
+    fields = (
+        jnp.where(alive, value_ref[0].astype(F32), 0.0),
+        (1.0 - lat_step) * (1.0 - lon_step),
+        (1.0 - lat_step) * lon_step,
+        lat_step * (1.0 - lon_step),
+        lat_step * lon_step,
+        (corner // 128).astype(F32),
+        (corner % 128).astype(F32),
+        channel_ref[0].astype(F32),
+    )
+    at_row = iota((8 * group, group), 0)
+    at_tile = iota((8 * group, group), 1)
+    by_row = jnp.zeros((8 * group, capacity), F32)
+    for i, field in enumerate(fields):
+        pick = jnp.where(at_row == at_tile * 8 + i, 1.0, 0.0).astype(BF16)
+        by_row = by_row + lax.dot_general(
+            pick, field.astype(BF16), (((1,), (1,)), ((), ())), preferred_element_type=F32
+        )
+    spots = lanes // capacity
+    spread = jnp.where(
+        iota((capacity, lanes), 1) == lax.rem(me, spots) * capacity + iota((capacity, lanes), 0),
+        1.0,
+        0.0,
+    ).astype(BF16)
+    packed[...] = dot(by_row.astype(BF16), spread).reshape(group, 8, lanes)
+    obs_in[me] = packed[me]
+
+    order_f = order_row[...].astype(F32)
+    order_col = column(order_f)
+    hot[...] = jnp.where(
+        iota((orders, orders), 1).astype(F32) == order_col, 1.0, 0.0
+    ).astype(BF16)
+    hot_t[...] = jnp.where(iota((orders, orders), 0) == order_row[...], 1.0, 0.0).astype(BF16)
+    factor = jnp.where(order_col == 0.0, 1.0, 2.0) * jnp.ones((1, lanes), F32)
+    factor_ref[...] = jnp.swapaxes(factor.reshape(group, chunks, CHUNK, lanes), 0, 1).reshape(
+        chunks, group * CHUNK, lanes
+    )
+
+    pl.semaphore_wait(barrier, group - 1)
     peers(
-        lambda peer, _: pl.semaphore_signal(
-            barrier, inc=1, device_id=place(peer), device_id_type=MESH
-        )
-    )
-    pl.semaphore_wait(barrier, group - 1)
-
-    peers(
-        lambda peer, _: send(
-            packed.at[peer], obs_in.at[me], obs_send.at[peer], obs_recv.at[me], peer
+        lambda peer: send(
+            packed.at[peer], obs_in.at[me], obs_send, obs_recv, place(peer)
         ).start()
     )
-    obs_in[me] = packed[me]
+    for copy in local[3:]:
+        copy.start()
 
     local[0].wait()
     for k in range(lat_dev):
@@ -364,64 +427,46 @@
         cdf = 0.5 * (1.0 + lax.erf(values * 0.7071067811865476))
         density = jnp.exp(-0.5 * values * values) * 0.3989422804014327
         slope_ref[k] = cdf + values * density
-    hot[...] = jnp.where(
-        lax.broadcasted_iota(jnp.int32, (orders, orders), 1) == order_col[...], 1.0, 0.0
-    ).astype(BF16)
-    hot_t[...] = jnp.where(
-        lax.broadcasted_iota(jnp.int32, (orders, orders), 0) == order_row[...], 1.0, 0.0
-    ).astype(BF16)
-    side = lat_count * CHUNK
-    first = lax.broadcasted_iota(jnp.int32, (side, side), 0)
-    second = lax.broadcasted_iota(jnp.int32, (side, side), 1)
-    to_lat[...] = jnp.where(
-        (first // CHUNK == second % lat_count) & (first % CHUNK == second // lat_count), 1.0, 0.0
-    ).astype(BF16)
-    to_slot[...] = jnp.where(
-        (second // CHUNK == first % lat_count) & (second % CHUNK == first // lat_count), 1.0, 0.0
-    ).astype(BF16)
     local[1].wait()
-    tile = 256
-
     for part in range(2):
 
         def make_tab(i, carry):
             at = pl.multiple_of(i * tile, tile)
-            got = dot(hot[...], table_ref[:, pl.ds(part * lon_count + at, tile)]).astype(BF16)
-            tab[:, part, :, pl.ds(at, tile)] = got.reshape(chunks, orders // chunks, tile)
+            got = dot(hot[...], table_ref[:, pl.ds(part * lon_count + at, tile)])
+            got = jnp.swapaxes(got.reshape(group, chunks, CHUNK, tile), 0, 1)
+            tab[:, part, :, pl.ds(at, tile)] = got.reshape(chunks, group * CHUNK, tile).astype(BF16)
             return carry
 
         lax.fori_loop(0, lon_count // tile, make_tab, 0)
 
     local[2].wait()
-    peers(
-        lambda peer, source: send(
-            packed.at[peer], obs_in.at[source], obs_send.at[peer], obs_recv.at[source], peer
-        ).wait()
-    )
-    lanes = obs_in.shape[2]
-    sources_per = lanes // capacity
+    send(
+        packed.at[pl.ds(0, group - 1)],
+        obs_in.at[pl.ds(0, group - 1)],
+        obs_send,
+        obs_recv,
+        beside,
+    ).wait_recv()
     halves = []
-    for h in range(group // sources_per):
-        halves.append(jnp.sum(obs_in[h * sources_per : (h + 1) * sources_per], axis=0))
+    for h in range(group // spots):
+        halves.append(jnp.sum(obs_in[h * spots : (h + 1) * spots], axis=0))
     seen = jnp.concatenate(halves, axis=1)
     received = seen.shape[1]
-    corner = seen[5:6].astype(jnp.int32)
-    channel = seen[6:7].astype(jnp.int32)
+    corner = seen[5:6].astype(jnp.int32) * 128 + seen[6:7].astype(jnp.int32)
+    channel = seen[7:8].astype(jnp.int32)
     left = corner % lon_count
     right = corner - left + (left + 1) % lon_count
     places = (corner, right, corner + lon_count, right + lon_count)
-    chan_ids = lax.axis_index("chan") * width + lax.broadcasted_iota(
-        jnp.int32, (width, received), 0
-    )
+    chan_ids = lax.axis_index("chan") * width + iota((width, received), 0)
     amounts = jnp.where(chan_ids == channel, seen[0:1], 0.0).astype(BF16)
     for k in range(lat_dev):
         for half in range(2):
             span = lon_count // 2
             begin = half * span
-            cells = k * lon_count + begin + lax.broadcasted_iota(jnp.int32, (span, received), 0)
+            cells = k * lon_count + begin + iota((span, received), 0)
             stencil = jnp.zeros((span, received), F32)
             for w, at in enumerate(places):
-                stencil = stencil + jnp.where(cells == at, seen[1 + w : 2 + w], 0.0)
+                stencil = jnp.where(cells == at, seen[1 + w : 2 + w], stencil)
             added = lax.dot_general(
                 stencil.astype(BF16), amounts, (((1,), (1,)), ((), ())), preferred_element_type=F32
             )
@@ -431,29 +476,44 @@
             pre_ref[here, k * width : (k + 1) * width] = (out_grad * slope_ref[k, here]).astype(BF16)
 
     def zonal(q, carry):
-        per = orders // chunks
-        at = pl.multiple_of(q * per, per)
-        factor = jnp.where(order_col[pl.ds(at, per), :] == 0, 1.0, 2.0)
+        scale = factor_ref[q][:, 0:1]
         for part in range(2):
-            got = (dot(tab[q, part], pre_ref[...]) * factor).reshape(group, CHUNK, lat_dev * width)
+            got = (dot(tab[q, part], pre_ref[...]) * scale).reshape(group, CHUNK, lat_dev * width)
             got = jnp.concatenate(
                 [got[:, :, k * width : (k + 1) * width] for k in range(lat_dev)], axis=1
             )
             fwd_out[q, :, :, part * width : (part + 1) * width] = got.astype(BF16)
         fwd_in[q, me] = fwd_out[q, me]
         peers(
-            lambda peer, _: send(
-                fwd_out.at[q, peer],
-                fwd_in.at[q, me],
-                fwd_send.at[q, peer],
-                fwd_recv.at[q, me],
-                peer,
+            lambda peer: send(
+                fwd_out.at[q, peer], fwd_in.at[q, me], fwd_send, fwd_recv.at[q], place(peer)
             ).start()
         )
         return carry
 
     lax.fori_loop(0, chunks, zonal, 0)
 
+    side = lat_count * CHUNK
+    first = iota((side, side), 0)
+    second = iota((side, side), 1)
+    to_lat[...] = jnp.where(
+        (first // CHUNK == second % lat_count) & (first % CHUNK == second // lat_count), 1.0, 0.0
+    ).astype(BF16)
+    to_slot[...] = jnp.where(
+        (second // CHUNK == first % lat_count) & (second % CHUNK == first // lat_count), 1.0, 0.0
+    ).astype(BF16)
+    joined = lanes // lat_count
+    for copy in local[4:]:
+        copy.wait()
+
+    def turn(j, carry):
+        table = leg_ref[pl.ds(j * joined, joined)].reshape(lanes, degrees)
+        leg_t[j] = table.T
+        return carry
+
+    lax.fori_loop(0, slot_dev // joined, turn, 0)
+    total[...] = jnp.zeros_like(total)
+    quad = column(quad_row[...])
     local[3].wait()
     for part in range(2):
 
@@ -464,61 +524,60 @@
             return carry
 
         lax.fori_loop(0, lon_count // tile, make_tab_t, 0)
-    total[...] = jnp.zeros_like(total)
-    for copy in local[4:]:
-        copy.wait()
+
+    span = 128
 
     def degrees_of(q, carry):
+        send(
+            fwd_out.at[q, pl.ds(0, group - 1)],
+            fwd_in.at[q, pl.ds(0, group - 1)],
+            fwd_send,
+            fwd_recv.at[q],
+            beside,
+        ).wait_recv()
+        arrived = dot(to_slot[...], fwd_in[q].reshape(side, 2 * width)).astype(BF16)
+        owner = iota((lanes, 2 * width), 0) // lat_count
+        for i in range(CHUNK):
+            begin = i // joined * lanes
+            by_slot[i] = jnp.where(
+                owner == i % joined, arrived[begin : begin + lanes].astype(F32), 0.0
+            ).astype(BF16)
+
+        def degree_tile(t, inner):
+            here = pl.ds(pl.multiple_of(t * span, span), span)
+            gain_real = gain_ref[0, here, :]
+            gain_imag = gain_ref[1, here, :]
+            sum_real = total[0, here, :]
+            sum_imag = total[1, here, :]
+            for i in range(CHUNK):
+                s = q * CHUNK + i
+                up = dot(leg_t[q * (CHUNK // joined) + i // joined, here, :], by_slot[i])
+                up_real = up[:, :width]
+                up_imag = up[:, width:]
+                saved_real = saved_ref[s, 0, here, :].astype(F32)
+                saved_imag = saved_ref[s, 1, here, :].astype(F32)
+                sum_real = sum_real + (up_real * saved_real + up_imag * saved_imag)
+                sum_imag = sum_imag + (up_imag * saved_real - up_real * saved_imag)
+                coeff_ref[i, here, :width] = (
+                    gain_real * up_real + gain_imag * up_imag
+                ).astype(BF16)
+                coeff_ref[i, here, width:] = (
+                    gain_real * up_imag - gain_imag * up_real
+                ).astype(BF16)
+            total[0, here, :] = sum_real
+            total[1, here, :] = sum_imag
+            return inner
+
+        lax.fori_loop(0, degrees // span, degree_tile, 0)
+        for i in range(CHUNK):
+            by_lat[i * lat_count : (i + 1) * lat_count, :] = (
+                dot(leg_ref[q * CHUNK + i], coeff_ref[i]) * quad
+            ).astype(BF16)
+        bwd_out[q] = dot(to_lat[...], by_lat[...]).astype(BF16).reshape(group, rows, 2 * width)
+        bwd_in[me, q] = bwd_out[q, me]
         peers(
-            lambda peer, source: send(
-                fwd_out.at[q, peer],
-                fwd_in.at[q, source],
-                fwd_send.at[q, peer],
-                fwd_recv.at[q, source],
-                peer,
-            ).wait()
-        )
-        arrived = fwd_in[q].reshape(side, 2 * width)
-        by_slot[...] = dot(to_slot[...], arrived).astype(BF16)
-
-        def per_slot(i, inner):
-            s = q * CHUNK + i
-            at = pl.multiple_of(i * lat_count, lat_count)
-            table = leg_ref[s]
-            up = lax.dot_general(
-                table,
-                by_slot[pl.ds(at, lat_count), :],
-                (((0,), (0,)), ((), ())),
-                preferred_element_type=F32,
-            )
-            up_real = up[:, :width]
-            up_imag = up[:, width:]
-            saved_real = saved_ref[s, 0].astype(F32)
-            saved_imag = saved_ref[s, 1].astype(F32)
-            total[0] += up_real * saved_real + up_imag * saved_imag
-            total[1] += up_imag * saved_real - up_real * saved_imag
-            gain_real = gain_ref[0]
-            gain_imag = gain_ref[1]
-            coeff = jnp.concatenate(
-                [
-                    (gain_real * up_real + gain_imag * up_imag).astype(BF16),
-                    (gain_real * up_imag - gain_imag * up_real).astype(BF16),
-                ],
-                axis=1,
-            )
-            by_lat[pl.ds(at, lat_count), :] = (dot(table, coeff) * quad_col[...]).astype(BF16)
-            return inner
-
-        lax.fori_loop(0, CHUNK, per_slot, 0)
-        bwd_out[q] = dot(to_lat[...], by_lat[...]).astype(BF16).reshape(group, rows, 2 * width)
-        bwd_in[q, me] = bwd_out[q, me]
-        peers(
-            lambda peer, _: send(
-                bwd_out.at[q, peer],
-                bwd_in.at[q, me],
-                bwd_send.at[q, peer],
-                bwd_recv.at[q, me],
-                peer,
+            lambda peer: send(
+                bwd_out.at[q, peer], bwd_in.at[me, q], bwd_send, bwd_recv, place(peer)
             ).start()
         )
         return carry
@@ -526,55 +585,89 @@
     lax.fori_loop(0, chunks, degrees_of, 0)
 
     share = degrees // group
+
+    def around(axis, size, mine, src, dst, sem):
+        def step(j, carry):
+            peer = lax.rem(mine + j, size)
+            send(
+                src.at[peer],
+                dst.at[mine],
+                sum_send.at[sem],
+                sum_recv.at[sem],
+                {axis: peer},
+            ).start()
+            return carry
+
+        lax.fori_loop(1, size, step, 0)
+
+    def landed(axis, size, mine, src, dst, sem):
+        return send(
+            src.at[pl.ds(0, size - 1)],
+            dst.at[pl.ds(0, size - 1)],
+            sum_send.at[sem],
+            sum_recv.at[sem],
+            {axis: lax.rem(mine + 1, size)},
+        )
+
+    stages = (
+        ("obs", obs_size, my_obs, near_out, near_in, 0),
+        ("lat", lat_size, my_lat, far_out, far_in, 1),
+        ("lat", lat_size, my_lat, far_out, far_in, 2),
+        ("obs", obs_size, my_obs, parts, parts, 3),
+    )
     for r in range(2):
-        part_out[:, r * share : (r + 1) * share, :] = (
-            total[r].reshape(group, share, width).astype(BF16)
-        )
-    part_in[me] = part_out[me]
-    peers(
-        lambda peer, _: send(
-            part_out.at[peer], part_in.at[me], part_send.at[peer], part_recv.at[me], peer
+        near_out[:, :, r * share : (r + 1) * share, :] = (
+            total[r].reshape(obs_size, lat_size, share, width).astype(BF16)
+        )
+    near_in[my_obs] = near_out[my_obs]
+    around(*stages[0])
+    landed(*stages[0]).wait_recv()
+    far_out[...] = jnp.sum(near_in[...].astype(F32), axis=0).astype(BF16)
+    far_in[my_lat] = far_out[my_lat]
+    around(*stages[1])
+    landed(*stages[1]).wait_recv()
+    parts[my_obs, my_lat] = jnp.sum(far_in[...].astype(F32), axis=0).astype(BF16)
+
+    def spread_out(j, carry):
+        peer = lax.rem(my_lat + j, lat_size)
+        send(
+            parts.at[my_obs, my_lat],
+            parts.at[my_obs, my_lat],
+            sum_send.at[2],
+            sum_recv.at[2],
+            {"lat": peer},
         ).start()
-    )
-
-    def lat_arrivals(q, carry):
-        peers(
-            lambda peer, source: send(
-                bwd_out.at[q, peer],
-                bwd_in.at[q, source],
-                bwd_send.at[q, peer],
-                bwd_recv.at[q, source],
-                peer,
-            ).wait()
-        )
         return carry
 
-    lax.fori_loop(0, chunks, lat_arrivals, 0)
-
-    peers(
-        lambda peer, source: send(
-            part_out.at[peer], part_in.at[source], part_send.at[peer], part_recv.at[source], peer
-        ).wait()
-    )
-    mine[...] = jnp.sum(part_in[...].astype(F32), axis=0).astype(BF16)
-    parts[me] = mine[...]
-    peers(
-        lambda peer, _: send(
-            mine, parts.at[me], full_send.at[peer], full_recv.at[me], peer
+    lax.fori_loop(1, lat_size, spread_out, 0)
+
+    send(
+        bwd_out.at[:, pl.ds(0, group - 1)],
+        bwd_in.at[pl.ds(0, group - 1)],
+        bwd_send,
+        bwd_recv,
+        beside,
+    ).wait_recv()
+    landed(*stages[2]).wait_recv()
+
+    def spread_wide(j, carry):
+        send(
+            parts.at[my_obs],
+            parts.at[my_obs],
+            sum_send.at[3],
+            sum_recv.at[3],
+            {"obs": lax.rem(my_obs + j, obs_size)},
         ).start()
-    )
-
-    back = bwd_in[...].astype(F32).reshape(chunks * group, lat_dev, CHUNK, 2 * width)
-    pieces = []
+        return carry
+
+    lax.fori_loop(1, obs_size, spread_wide, 0)
+
+    back = bwd_in[...].astype(F32).reshape(group * chunks, lat_dev, CHUNK, 2 * width)
     for part in range(2):
         lane = slice(part * width, (part + 1) * width)
-        pieces.append(
-            jnp.concatenate(
-                [back[:, k, :, lane].reshape(orders, width) for k in range(lat_dev)], axis=1
-            ).astype(BF16)
-        )
-    grads = jnp.concatenate(pieces, axis=0)
-    pre_ref[0 : 2 * orders, :] = grads
+        pre_ref[part * orders : (part + 1) * orders, :] = jnp.concatenate(
+            [back[:, k, :, lane].reshape(orders, width) for k in range(lat_dev)], axis=1
+        ).astype(BF16)
 
     def to_grid(i, carry):
         at = pl.multiple_of(i * tile, tile)
@@ -587,15 +680,33 @@
 
     lax.fori_loop(0, lon_count // tile, to_grid, 0)
 
-    peers(
-        lambda peer, source: send(
-            mine, parts.at[source], full_send.at[peer], full_recv.at[source], peer
-        ).wait()
-    )
+    landed(*stages[3]).wait_recv()
     for r in range(2):
         gain_out[r] = (
-            parts[:, r * share : (r + 1) * share, :].astype(F32).reshape(degrees, width)
-        )
+            parts[:, :, r * share : (r + 1) * share, :].astype(F32).reshape(degrees, width)
+        )
+
+    send(
+        packed.at[pl.ds(0, group - 1)], obs_in.at[pl.ds(0, group - 1)], obs_send, obs_recv, beside
+    ).wait_send()
+    send(
+        fwd_out.at[:, pl.ds(0, group - 1)],
+        fwd_in.at[:, pl.ds(0, group - 1)],
+        fwd_send,
+        fwd_recv.at[0],
+        beside,
+    ).wait_send()
+    send(
+        bwd_out.at[:, pl.ds(0, group - 1)],
+        bwd_in.at[pl.ds(0, group - 1)],
+        bwd_send,
+        bwd_recv,
+        beside,
+    ).wait_send()
+    landed(*stages[0]).wait_send()
+    landed(*stages[1]).wait_send()
+    landed(*stages[2]).wait_send()
+    landed(*stages[3]).wait_send()
 
 
 def on_device(
@@ -619,36 +730,11 @@
     group = lat_size * obs_size
     slot_dev, degrees, lat_count = legendre.shape
     orders = order_slots.shape[0]
-    capacity = obs_value.shape[1]
     chunks = slot_dev // CHUNK
     rows = CHUNK * lat_dev
     lanes = 128
     side = lat_count * CHUNK
-
-    me = lax.axis_index("lat") * obs_size + lax.axis_index("obs")
-    alive_slots = lax.iota(jnp.int32, capacity)[:, None] < slot_counts[0][None, :]
-    amounts = jnp.where(alive_slots, obs_value[0], jnp.zeros((), BF16)).astype(F32)
-    lat_step = obs_lat_frac[0].astype(F32)
-    lon_step = obs_lon_frac[0].astype(F32)
-    weights = (
-        (1.0 - lat_step) * (1.0 - lon_step),
-        (1.0 - lat_step) * lon_step,
-        lat_step * (1.0 - lon_step),
-        lat_step * lon_step,
-    )
-    fields = jnp.stack(
-        [amounts]
-        + [lax.reduce_precision(w, 8, 7) for w in weights]
-        + [obs_corner[0].astype(F32), obs_channel[0].astype(F32), jnp.zeros_like(amounts)]
-    )
-    spots = lanes // capacity
-    fields = jnp.transpose(fields, (2, 0, 1))
-    packed = jnp.where(
-        (lax.iota(jnp.int32, lanes) // capacity == me % spots)[None, None, :],
-        jnp.tile(fields, (1, 1, spots)),
-        0.0,
-    )
-    order_q = jnp.transpose(order_slots.reshape(group, chunks, CHUNK), (1, 0, 2)).reshape(orders)
+    joined = lanes // lat_count
     table = base_tables(orders, lon_count)
     table_t = np.ascontiguousarray(table.T)
 
@@ -657,12 +743,12 @@
     dma = pltpu.SemaphoreType.DMA
     share = degrees // group
     return pl.pallas_call(
-        functools.partial(block_kernel, lat_size, obs_size, capacity),
+        functools.partial(block_kernel, lat_size, obs_size),
         out_shape=(
             jax.ShapeDtypeStruct((lat_dev, lon_count, width), BF16),
             jax.ShapeDtypeStruct((2, degrees, width), F32),
         ),
-        in_specs=[vmem] * 4 + [anywhere] * 7,
+        in_specs=[vmem] * 8 + [anywhere] * 7,
         out_specs=(vmem, vmem),
         scratch_shapes=[
             pltpu.VMEM((lat_dev, lon_count, width), BF16),
@@ -673,10 +759,13 @@
             pltpu.VMEM((orders, 2 * lon_count), BF16),
             pltpu.VMEM((2 * lon_count, orders), BF16),
             pltpu.VMEM((group, 8, lanes), F32),
+            pltpu.VMEM((group, 8, lanes), F32),
             pltpu.VMEM((orders, orders), BF16),
             pltpu.VMEM((orders, orders), BF16),
+            pltpu.VMEM((chunks, group * CHUNK, lanes), F32),
             pltpu.VMEM((chunks, 2, orders // chunks, lon_count), BF16),
             pltpu.VMEM((lon_count, 2 * orders), BF16),
+            pltpu.VMEM((slot_dev // joined, degrees, lanes), BF16),
             pltpu.VMEM((side, side), BF16),
             pltpu.VMEM((side, side), BF16),
             pltpu.VMEM((lat_dev, lon_count, width), F32),
@@ -684,36 +773,40 @@
             pltpu.VMEM((max(lon_count, 2 * orders), lat_dev * width), BF16),
             pltpu.VMEM((chunks, group, rows, 2 * width), BF16),
             pltpu.VMEM((chunks, group, rows, 2 * width), BF16),
-            pltpu.VMEM((side, 2 * width), BF16),
+            pltpu.VMEM((CHUNK, lanes, 2 * width), BF16),
+            pltpu.VMEM((CHUNK, degrees, 2 * width), BF16),
             pltpu.VMEM((side, 2 * width), BF16),
             pltpu.VMEM((chunks, group, rows, 2 * width), BF16),
-            pltpu.VMEM((chunks, group, rows, 2 * width), BF16),
+            pltpu.VMEM((group, chunks, rows, 2 * width), BF16),
             pltpu.VMEM((2, degrees, width), F32),
-            pltpu.VMEM((group, 2 * share, width), BF16),
-            pltpu.VMEM((group, 2 * share, width), BF16),
-            pltpu.VMEM((2 * share, width), BF16),
-            pltpu.VMEM((group, 2 * share, width), BF16),
+            pltpu.VMEM((obs_size, lat_size, 2 * share, width), BF16),
+            pltpu.VMEM((obs_size, lat_size, 2 * share, width), BF16),
+            pltpu.VMEM((lat_size, 2 * share, width), BF16),
+            pltpu.VMEM((lat_size, 2 * share, width), BF16),
+            pltpu.VMEM((obs_size, lat_size, 2 * share, width), BF16),
             dma((7,)),
-            dma((group,)),
-            dma((group,)),
-            dma((chunks, group)),
-            dma((chunks, group)),
-            dma((chunks, group)),
-            dma((chunks, group)),
-            dma((group,)),
-            dma((group,)),
-            dma((group,)),
-            dma((group,)),
+            dma,
+            dma,
+            dma,
+            dma((chunks,)),
+            dma,
+            dma,
+            dma((4,)),
+            dma((4,)),
         ],
         compiler_params=pltpu.CompilerParams(
-            collective_id=0, has_side_effects=True, vmem_limit_bytes=50 * 1024 * 1024
+            collective_id=0, has_side_effects=True, vmem_limit_bytes=60 * 1024 * 1024
         ),
         name="block_backward",
     )(
-        packed,
-        order_q[:, None],
-        order_q[None, :],
-        quad_weights[:, None],
+        obs_value,
+        obs_lat_frac,
+        obs_lon_frac,
+        obs_corner,
+        obs_channel,
+        slot_counts,
+        order_slots[None, :],
+        quad_weights[None, :],
         next_grad,
         pre_act,
         jnp.transpose(legendre, (0, 2, 1)),
@@ -724,7 +817,8 @@
     )
 
 
-def kernel_fits(next_grad, legendre, obs_value, group):
+def kernel_fits(next_grad, legendre, obs_value, lat_size, obs_size):
+    group = lat_size * obs_size
     lat_dev, lon_count, width = next_grad.shape
     slot_dev, degrees, lat_count = legendre.shape
     capacity = obs_value.shape[1]
@@ -732,6 +826,11 @@
         slot_dev % CHUNK == 0
         and (CHUNK * lat_dev) % 16 == 0
         and lat_count * CHUNK <= 512
+        and 128 % lat_count == 0
+        and CHUNK % (128 // lat_count) == 0
+        and degrees % 128 == 0
+        and lat_size > 1
+        and obs_size > 1
         and width % 128 == 0
         and lon_count % 512 == 0
         and degrees % (16 * group) == 0
@@ -741,8 +840,7 @@
 
 
 def device_path(*args):
-    group = lax.axis_size("lat") * lax.axis_size("obs")
-    if kernel_fits(args[0], args[2], args[7], group):
+    if kernel_fits(args[0], args[2], args[7], lax.axis_size("lat"), lax.axis_size("obs")):
         return on_device(*args)
     return plain_path(*args)
 

time: 67.7 us -> 55.3 us (0.82)
  other arithmetic: 4.94 us -> 0 us
  Pallas kernels: 55.6 us -> 50.7 us
  local copies, waits for them, and re-layouts: 5.84 us -> 3.74 us
    pallas_call x1, Pallas kernels: 55.6 us -> 50.7 us  [on_device(): pl.pallas_call(functools.partial(block_kernel, lat_size, obs_size), out_s...]
    unnamed x7 -> x0, other arithmetic: 4.93 us -> none
    broadcast_in_dim x1 -> x0, local copies, waits for them, and re-layouts: 0.85 us -> none  [on_device(): quad_weights[:, None]]
    reshape x1 -> x0, local copies, waits for them, and re-layouts: 0.78 us -> none  [on_device(): order_slots.reshape(group, chunks, CHUNK)]
    unnamed x10 -> x2, local copies, waits for them, and re-layouts: 3.67 us -> 3.74 us
where the time goes in v2:
time: 55.3 us; the launch traced here: 55 us
  Pallas kernels  50.7 us (92%)
  local copies, waits for them, and re-layouts  3.74 us (7%)
  between operations  0.64 us (1%)
    pallas_call x1, Pallas kernels, on_device(): pl.pallas_call(functools.partial(block_kernel, lat_size, obs_size), out_s...  50.7 us
    unnamed x2, local copies, waits for them, and re-layouts  3.74 us

profile of v2, /device:TPU:0, one launch (start us, length us, event | category | flops | bytes accessed | tf_op | source)
XLA Modules:
  0.0 55.0 jit_solution(5212782541236330399)
XLA Ops:
  0.6 50.7 %block_backward.1 = (bf16[2,1024,128]{2,1,0:T(8,128)(2,1)}, f32[2,512,128]{2,1,0:T(8,128)}) custom-call(bf16[1,16,16]{2,1,0:T(8,128)(2,1)} %value_ref.1, bf16[1,16,16]{2,1,0:T(8,128)(2,1)} %lat_frac_ref.1, bf16[1,16,16]{2,1,0:T(8,128)(2,1)} %lon_frac_ref.1, s32[1,16,16]{2,1,0:T(8,128)} %corner_ref.1, s32[1,16,16]{2,1,0:T(8,128)} %channel_ref.1, ...), custom_call_target="tpu_custom_call" | custom-call | tf_op jit(solution)/shard_map/block_backward/pallas_call | solution.py:745
  51.3 1.9 %copy.19 = bf16[2,1024,128]{2,1,0:T(8,128)(2,1)} copy(bf16[2,1024,128]{2,1,0:T(8,128)(2,1)} %get-tuple-element.4) | data formatting | bytes 1048576
  53.2 1.9 %copy.20 = f32[2,512,128]{2,1,0:T(8,128)} copy(f32[2,512,128]{2,1,0:T(8,128)} %get-tuple-element.5) | data formatting | bytes 1048576

commit v3 on v2

--- a/solution.py
+++ b/solution.py
@@ -272,8 +272,7 @@
     obs_in,
     hot,
     hot_t,
-    factor_ref,
-    tab,
+    waves,
     tab_t,
     leg_t,
     to_slot,
@@ -317,15 +316,15 @@
     lanes = packed.shape[2]
     tile = 256
 
-    def place(peer):
-        return {"lat": peer // obs_size, "obs": peer % obs_size}
+    others = []
+    for j in range(1, group):
+        lat_at = lax.rem(my_lat + j // obs_size, lat_size)
+        obs_at = lax.rem(my_obs + j % obs_size, obs_size)
+        others.append((lat_at * obs_size + obs_at, {"lat": lat_at, "obs": obs_at}))
 
     def peers(body):
-        def step(j, carry):
-            body(lax.rem(me + j, group))
-            return carry
-
-        lax.fori_loop(1, group, step, 0)
+        for peer, where in others:
+            body(peer, where)
 
     def send(src, dst, send_sem, recv_sem, target):
         return pltpu.make_async_remote_copy(
@@ -349,8 +348,8 @@
 
     barrier = pltpu.get_barrier_semaphore()
     peers(
-        lambda peer: pl.semaphore_signal(
-            barrier, inc=1, device_id=place(peer), device_id_type=MESH
+        lambda _, where: pl.semaphore_signal(
+            barrier, inc=1, device_id=where, device_id_type=MESH
         )
     )
     local = [
@@ -402,20 +401,16 @@
     obs_in[me] = packed[me]
 
     order_f = order_row[...].astype(F32)
-    order_col = column(order_f)
-    hot[...] = jnp.where(
-        iota((orders, orders), 1).astype(F32) == order_col, 1.0, 0.0
-    ).astype(BF16)
-    hot_t[...] = jnp.where(iota((orders, orders), 0) == order_row[...], 1.0, 0.0).astype(BF16)
-    factor = jnp.where(order_col == 0.0, 1.0, 2.0) * jnp.ones((1, lanes), F32)
-    factor_ref[...] = jnp.swapaxes(factor.reshape(group, chunks, CHUNK, lanes), 0, 1).reshape(
-        chunks, group * CHUNK, lanes
-    )
+    order_col = column(order_f).reshape(group, chunks, CHUNK, 1)
+    per = orders // chunks
+    for q in range(chunks):
+        here = order_col[:, q].reshape(per, 1)
+        hot[q] = jnp.where(iota((per, orders), 1).astype(F32) == here, 1.0, 0.0).astype(BF16)
 
     pl.semaphore_wait(barrier, group - 1)
     peers(
-        lambda peer: send(
-            packed.at[peer], obs_in.at[me], obs_send, obs_recv, place(peer)
+        lambda peer, where: send(
+            packed.at[peer], obs_in.at[me], obs_send, obs_recv, where
         ).start()
     )
     for copy in local[3:]:
@@ -427,18 +422,6 @@
         cdf = 0.5 * (1.0 + lax.erf(values * 0.7071067811865476))
         density = jnp.exp(-0.5 * values * values) * 0.3989422804014327
         slope_ref[k] = cdf + values * density
-    local[1].wait()
-    for part in range(2):
-
-        def make_tab(i, carry):
-            at = pl.multiple_of(i * tile, tile)
-            got = dot(hot[...], table_ref[:, pl.ds(part * lon_count + at, tile)])
-            got = jnp.swapaxes(got.reshape(group, chunks, CHUNK, tile), 0, 1)
-            tab[:, part, :, pl.ds(at, tile)] = got.reshape(chunks, group * CHUNK, tile).astype(BF16)
-            return carry
-
-        lax.fori_loop(0, lon_count // tile, make_tab, 0)
-
     local[2].wait()
     send(
         packed.at[pl.ds(0, group - 1)],
@@ -475,18 +458,25 @@
             out_ref[k, here] = out_grad
             pre_ref[here, k * width : (k + 1) * width] = (out_grad * slope_ref[k, here]).astype(BF16)
 
+    local[1].wait()
+    factor = jnp.where(iota((orders, 1), 0) == 0, 1.0, 2.0)
+    for part in range(2):
+        got = dot(table_ref[:, part * lon_count : (part + 1) * lon_count], pre_ref[...])
+        for k in range(lat_dev):
+            begin = (k * 2 + part) * width
+            waves[:, begin : begin + width] = (
+                got[:, k * width : (k + 1) * width] * factor
+            ).astype(BF16)
+
     def zonal(q, carry):
-        scale = factor_ref[q][:, 0:1]
-        for part in range(2):
-            got = (dot(tab[q, part], pre_ref[...]) * scale).reshape(group, CHUNK, lat_dev * width)
-            got = jnp.concatenate(
-                [got[:, :, k * width : (k + 1) * width] for k in range(lat_dev)], axis=1
-            )
-            fwd_out[q, :, :, part * width : (part + 1) * width] = got.astype(BF16)
+        got = dot(hot[q], waves[...]).reshape(group, CHUNK, lat_dev * 2 * width)
+        fwd_out[q] = jnp.concatenate(
+            [got[:, :, k * 2 * width : (k + 1) * 2 * width] for k in range(lat_dev)], axis=1
+        ).astype(BF16)
         fwd_in[q, me] = fwd_out[q, me]
         peers(
-            lambda peer: send(
-                fwd_out.at[q, peer], fwd_in.at[q, me], fwd_send, fwd_recv.at[q], place(peer)
+            lambda peer, where: send(
+                fwd_out.at[q, peer], fwd_in.at[q, me], fwd_send, fwd_recv.at[q], where
             ).start()
         )
         return carry
@@ -514,16 +504,15 @@
     lax.fori_loop(0, slot_dev // joined, turn, 0)
     total[...] = jnp.zeros_like(total)
     quad = column(quad_row[...])
-    local[3].wait()
-    for part in range(2):
-
-        def make_tab_t(i, carry):
+
+    def make_tab_t(part):
+        def step(i, carry):
             at = pl.multiple_of(i * tile, tile)
             got = dot(table_t_ref[pl.ds(part * lon_count + at, tile), :], hot_t[...])
             tab_t[pl.ds(at, tile), part * orders : (part + 1) * orders] = got.astype(BF16)
             return carry
 
-        lax.fori_loop(0, lon_count // tile, make_tab_t, 0)
+        lax.fori_loop(0, lon_count // tile, step, 0)
 
     span = 128
 
@@ -576,8 +565,8 @@
         bwd_out[q] = dot(to_lat[...], by_lat[...]).astype(BF16).reshape(group, rows, 2 * width)
         bwd_in[me, q] = bwd_out[q, me]
         peers(
-            lambda peer: send(
-                bwd_out.at[q, peer], bwd_in.at[me, q], bwd_send, bwd_recv, place(peer)
+            lambda peer, where: send(
+                bwd_out.at[q, peer], bwd_in.at[me, q], bwd_send, bwd_recv, where
             ).start()
         )
         return carry
@@ -621,10 +610,14 @@
         )
     near_in[my_obs] = near_out[my_obs]
     around(*stages[0])
+    hot_t[...] = jnp.where(iota((orders, orders), 0) == order_row[...], 1.0, 0.0).astype(BF16)
+    local[3].wait()
+    make_tab_t(0)
     landed(*stages[0]).wait_recv()
     far_out[...] = jnp.sum(near_in[...].astype(F32), axis=0).astype(BF16)
     far_in[my_lat] = far_out[my_lat]
     around(*stages[1])
+    make_tab_t(1)
     landed(*stages[1]).wait_recv()
     parts[my_obs, my_lat] = jnp.sum(far_in[...].astype(F32), axis=0).astype(BF16)
 
@@ -739,7 +732,7 @@
     table_t = np.ascontiguousarray(table.T)
 
     vmem = pl.BlockSpec(memory_space=pltpu.VMEM)
-    anywhere = pl.BlockSpec(memory_space=pl.ANY)
+    anywhere = pl.BlockSpec(memory_space=pltpu.HBM)
     dma = pltpu.SemaphoreType.DMA
     share = degrees // group
     return pl.pallas_call(
@@ -760,10 +753,9 @@
             pltpu.VMEM((2 * lon_count, orders), BF16),
             pltpu.VMEM((group, 8, lanes), F32),
             pltpu.VMEM((group, 8, lanes), F32),
+            pltpu.VMEM((chunks, orders // chunks, orders), BF16),
             pltpu.VMEM((orders, orders), BF16),
-            pltpu.VMEM((orders, orders), BF16),
-            pltpu.VMEM((chunks, group * CHUNK, lanes), F32),
-            pltpu.VMEM((chunks, 2, orders // chunks, lon_count), BF16),
+            pltpu.VMEM((orders, lat_dev * 2 * width), BF16),
             pltpu.VMEM((lon_count, 2 * orders), BF16),
             pltpu.VMEM((slot_dev // joined, degrees, lanes), BF16),
             pltpu.VMEM((side, side), BF16),
@@ -795,7 +787,7 @@
             dma((4,)),
         ],
         compiler_params=pltpu.CompilerParams(
-            collective_id=0, has_side_effects=True, vmem_limit_bytes=60 * 1024 * 1024
+            collective_id=0, has_side_effects=True, vmem_limit_bytes=44 * 1024 * 1024
         ),
         name="block_backward",
     )(

time: 55.3 us -> 65.4 us (1.18)
  local copies, waits for them, and re-layouts: 3.74 us -> 14.6 us
  Pallas kernels: 50.7 us -> 49.6 us
    unnamed x2 -> x30, local copies, waits for them, and re-layouts: 3.74 us -> 14.6 us
    pallas_call x1, Pallas kernels: 50.7 us -> 49.6 us  [on_device(): pl.pallas_call(functools.partial(block_kernel, lat_size, obs_size), out_s...]
where the time goes in v3:
time: 65.4 us; the launch traced here: 64.9 us
  Pallas kernels  49.6 us (76%)
  local copies, waits for them, and re-layouts  14.6 us (22%)
  between operations  0.67 us (1%)
    pallas_call x1, Pallas kernels, on_device(): pl.pallas_call(functools.partial(block_kernel, lat_size, obs_size), out_s...  49.6 us
    unnamed x30, local copies, waits for them, and re-layouts  14.6 us

profile of v3, /device:TPU:0, one launch (start us, length us, event | category | flops | bytes accessed | tf_op | source)
XLA Modules:
  0.0 64.9 jit_solution(6680609024259751366)
XLA Ops:
  0.6 0.0 copy-start
  0.6 1.6 %copy-done = bf16[2048,512]{1,0:T(8,128)(2,1)S(1)} copy-done((bf16[2048,512]{1,0:T(8,128)(2,1)S(1)}, bf16[2048,512]{1,0:T(8,128)(2,1)}, u32[]{:S(2)}) %copy-start) | copy-done | bytes 2097176
  2.2 0.0 copy-start.1
  2.2 1.6 %copy-done.1 = bf16[512,2048]{1,0:T(8,128)(2,1)S(1)} copy-done((bf16[512,2048]{1,0:T(8,128)(2,1)S(1)}, bf16[512,2048]{1,0:T(8,128)(2,1)}, u32[]{:S(2)}) %copy-start.1) | copy-done | bytes 2097176
  3.8 0.0 copy-start.2
  3.8 1.2 %copy-done.2 = bf16[32,512,32]{1,2,0:T(8,128)(2,1)S(1)} copy-done((bf16[32,512,32]{1,2,0:T(8,128)(2,1)S(1)}, bf16[32,512,32]{1,2,0:T(8,128)(2,1)}, u32[]{:S(2)}) %copy-start.2) | copy-done | bytes 1048600
  5.0 0.0 copy-start.3
  5.0 1.0 %copy-done.3 = bf16[2,1024,128]{2,1,0:T(8,128)(2,1)S(1)} copy-done((bf16[2,1024,128]{2,1,0:T(8,128)(2,1)S(1)}, bf16[2,1024,128]{2,1,0:T(8,128)(2,1)}, u32[]{:S(2)}) %copy-start.3) | copy-done | bytes 524312
  6.1 0.0 copy-start.4
  6.1 1.0 %copy-done.4 = bf16[2,1024,128]{2,1,0:T(8,128)(2,1)S(1)} copy-done((bf16[2,1024,128]{2,1,0:T(8,128)(2,1)S(1)}, bf16[2,1024,128]{2,1,0:T(8,128)(2,1)}, u32[]{:S(2)}) %copy-start.4) | copy-done | bytes 524312
  7.1 0.0 copy-start.5
  7.1 1.0 %copy-done.5 = f32[2,512,128]{2,1,0:T(8,128)S(1)} copy-done((f32[2,512,128]{2,1,0:T(8,128)S(1)}, f32[2,512,128]{2,1,0:T(8,128)}, u32[]{:S(2)}) %copy-start.5) | copy-done | bytes 524312
  8.2 0.0 copy-start.6
  8.2 0.7 %copy-done.6 = s32[1,16,16]{2,1,0:T(8,128)S(1)} copy-done((s32[1,16,16]{2,1,0:T(8,128)S(1)}, s32[1,16,16]{2,1,0:T(8,128)}, u32[]{:S(2)}) %copy-start.6) | copy-done | bytes 1048
  8.9 0.0 copy-start.7
  8.9 0.7 %copy-done.7 = s32[1,16,16]{2,1,0:T(8,128)S(1)} copy-done((s32[1,16,16]{2,1,0:T(8,128)S(1)}, s32[1,16,16]{2,1,0:T(8,128)}, u32[]{:S(2)}) %copy-start.7) | copy-done | bytes 1048
  9.6 0.0 copy-start.8
  9.6 0.7 %copy-done.8 = bf16[1,16,16]{2,1,0:T(8,128)(2,1)S(1)} copy-done((bf16[1,16,16]{2,1,0:T(8,128)(2,1)S(1)}, bf16[1,16,16]{2,1,0:T(8,128)(2,1)}, u32[]{:S(2)}) %copy-start.8) | copy-done | bytes 536
  10.3 0.0 copy-start.9
  10.3 0.7 %copy-done.9 = bf16[1,16,16]{2,1,0:T(8,128)(2,1)S(1)} copy-done((bf16[1,16,16]{2,1,0:T(8,128)(2,1)S(1)}, bf16[1,16,16]{2,1,0:T(8,128)(2,1)}, u32[]{:S(2)}) %copy-start.9) | copy-done | bytes 536
  10.9 0.0 copy-start.10
  10.9 0.7 %copy-done.10 = bf16[1,16,16]{2,1,0:T(8,128)(2,1)S(1)} copy-done((bf16[1,16,16]{2,1,0:T(8,128)(2,1)S(1)}, bf16[1,16,16]{2,1,0:T(8,128)(2,1)}, u32[]{:S(2)}) %copy-start.10) | copy-done | bytes 536
  11.6 0.0 copy-start.11
  11.6 0.7 %copy-done.11 = s32[512]{0:T(512)S(1)} copy-done((s32[512]{0:T(512)S(1)}, s32[512]{0:T(512)}, u32[]{:S(2)}) %copy-start.11) | copy-done | bytes 2072
  12.3 0.0 copy-start.12
  12.3 0.7 %copy-done.12 = s32[1,16]{1,0:T(1,128)S(1)} copy-done((s32[1,16]{1,0:T(1,128)S(1)}, s32[1,16]{1,0:T(1,128)}, u32[]{:S(2)}) %copy-start.12) | copy-done | bytes 88
  13.0 0.0 copy-start.13
  13.0 0.7 %copy-done.13 = f32[32]{0:T(128)S(1)} copy-done((f32[32]{0:T(128)S(1)}, f32[32]{0:T(128)}, u32[]{:S(2)}) %copy-start.13) | copy-done | bytes 152
  13.6 49.6 %block_backward.1 = (bf16[2,1024,128]{2,1,0:T(8,128)(2,1)S(1)}, f32[2,512,128]{2,1,0:T(8,128)S(1)}) custom-call(bf16[1,16,16]{2,1,0:T(8,128)(2,1)S(1)} %copy-done.8, bf16[1,16,16]{2,1,0:T(8,128)(2,1)S(1)} %copy-done.9, bf16[1,16,16]{2,1,0:T(8,128)(2,1)S(1)} %copy-done.10, s32[1,16,16]{2,1,0:T(8,128)S(1)} %copy-done.6, s32[1,16,16]{2,1,0:T(8,128)S(1)} %copy-done.7, ...), custom_call_target="tpu_custom_call" | custom-call | tf_op jit(solution)/shard_map/block_backward/pallas_call | solution.py:738
  63.3 0.8 %copy.19 = bf16[2,1024,128]{2,1,0:T(8,128)(2,1)} copy(bf16[2,1024,128]{2,1,0:T(8,128)(2,1)S(1)} %get-tuple-element.4) | data formatting | bytes 1048576
  64.1 0.8 %copy.20 = f32[2,512,128]{2,1,0:T(8,128)} copy(f32[2,512,128]{2,1,0:T(8,128)S(1)} %get-tuple-element.5) | data formatting | bytes 1048576
Async XLA Ops:
  0.6 1.6 %copy-start = (bf16[2048,512]{1,0:T(8,128)(2,1)S(1)}, bf16[2048,512]{1,0:T(8,128)(2,1)}, u32[]{:S(2)}) copy-start(bf16[2048,512]{1,0:T(8,128)(2,1)} %constant.5.clone.table_t_hbm) | copy-start | bytes 6291460
  2.2 1.6 %copy-start.1 = (bf16[512,2048]{1,0:T(8,128)(2,1)S(1)}, bf16[512,2048]{1,0:T(8,128)(2,1)}, u32[]{:S(2)}) copy-start(bf16[512,2048]{1,0:T(8,128)(2,1)} %constant.4.clone.table_hbm) | copy-start | bytes 6291460
  3.8 1.2 %copy-start.2 = (bf16[32,512,32]{1,2,0:T(8,128)(2,1)S(1)}, bf16[32,512,32]{1,2,0:T(8,128)(2,1)}, u32[]{:S(2)}) copy-start(bf16[32,512,32]{1,2,0:T(8,128)(2,1)} %param.17) | copy-start | bytes 3145732
  5.0 1.0 %copy-start.3 = (bf16[2,1024,128]{2,1,0:T(8,128)(2,1)S(1)}, bf16[2,1024,128]{2,1,0:T(8,128)(2,1)}, u32[]{:S(2)}) copy-start(bf16[2,1024,128]{2,1,0:T(8,128)(2,1)} %next_hbm.1) | copy-start | bytes 1572868
  6.1 1.0 %copy-start.4 = (bf16[2,1024,128]{2,1,0:T(8,128)(2,1)S(1)}, bf16[2,1024,128]{2,1,0:T(8,128)(2,1)}, u32[]{:S(2)}) copy-start(bf16[2,1024,128]{2,1,0:T(8,128)(2,1)} %act_hbm.1) | copy-start | bytes 1572868
  7.1 1.0 %copy-start.5 = (f32[2,512,128]{2,1,0:T(8,128)S(1)}, f32[2,512,128]{2,1,0:T(8,128)}, u32[]{:S(2)}) copy-start(f32[2,512,128]{2,1,0:T(8,128)} %gain_hbm.1) | copy-start | bytes 1572868
  8.2 0.7 %copy-start.6 = (s32[1,16,16]{2,1,0:T(8,128)S(1)}, s32[1,16,16]{2,1,0:T(8,128)}, u32[]{:S(2)}) copy-start(s32[1,16,16]{2,1,0:T(8,128)} %corner_ref.1) | copy-start | bytes 3076
  8.9 0.7 %copy-start.7 = (s32[1,16,16]{2,1,0:T(8,128)S(1)}, s32[1,16,16]{2,1,0:T(8,128)}, u32[]{:S(2)}) copy-start(s32[1,16,16]{2,1,0:T(8,128)} %channel_ref.1) | copy-start | bytes 3076
  9.6 0.7 %copy-start.8 = (bf16[1,16,16]{2,1,0:T(8,128)(2,1)S(1)}, bf16[1,16,16]{2,1,0:T(8,128)(2,1)}, u32[]{:S(2)}) copy-start(bf16[1,16,16]{2,1,0:T(8,128)(2,1)} %value_ref.1) | copy-start | bytes 1540
  10.3 0.7 %copy-start.9 = (bf16[1,16,16]{2,1,0:T(8,128)(2,1)S(1)}, bf16[1,16,16]{2,1,0:T(8,128)(2,1)}, u32[]{:S(2)}) copy-start(bf16[1,16,16]{2,1,0:T(8,128)(2,1)} %lat_frac_ref.1) | copy-start | bytes 1540
  10.9 0.7 %copy-start.10 = (bf16[1,16,16]{2,1,0:T(8,128)(2,1)S(1)}, bf16[1,16,16]{2,1,0:T(8,128)(2,1)}, u32[]{:S(2)}) copy-start(bf16[1,16,16]{2,1,0:T(8,128)(2,1)} %lon_frac_ref.1) | copy-start | bytes 1540
  11.6 0.7 %copy-start.11 = (s32[512]{0:T(512)S(1)}, s32[512]{0:T(512)}, u32[]{:S(2)}) copy-start(s32[512]{0:T(512)} %param.18) | copy-start | bytes 6148
  12.3 0.7 %copy-start.12 = (s32[1,16]{1,0:T(1,128)S(1)}, s32[1,16]{1,0:T(1,128)}, u32[]{:S(2)}) copy-start(s32[1,16]{1,0:T(1,128)} %count_ref.1) | copy-start | bytes 196
  13.0 0.7 %copy-start.13 = (f32[32]{0:T(128)S(1)}, f32[32]{0:T(128)}, u32[]{:S(2)}) copy-start(f32[32]{0:T(128)} %param.19) | copy-start | bytes 388

commit v4 on v3

--- a/solution.py
+++ b/solution.py
@@ -287,6 +287,7 @@
     by_lat,
     bwd_out,
     bwd_in,
+    grid_ref,
     total,
     near_out,
     near_in,
@@ -302,6 +303,7 @@
     bwd_recv,
     sum_send,
     sum_recv,
+    leave_sem,
 ):
     group = lat_size * obs_size
     my_lat = lax.axis_index("lat")
@@ -514,6 +516,45 @@
 
         lax.fori_loop(0, lon_count // tile, step, 0)
 
+    share = degrees // group
+
+    def around(axis, size, mine, src, dst, sem):
+        def step(j, carry):
+            peer = lax.rem(mine + j, size)
+            send(
+                src.at[peer],
+                dst.at[mine],
+                sum_send.at[sem],
+                sum_recv.at[sem],
+                {axis: peer},
+            ).start()
+            return carry
+
+        lax.fori_loop(1, size, step, 0)
+
+    def landed(axis, size, mine, src, dst, sem):
+        return send(
+            src.at[pl.ds(0, size - 1)],
+            dst.at[pl.ds(0, size - 1)],
+            sum_send.at[sem],
+            sum_recv.at[sem],
+            {axis: lax.rem(mine + 1, size)},
+        )
+
+    stages = (
+        ("obs", obs_size, my_obs, near_out, near_in, 0),
+        ("lat", lat_size, my_lat, far_out, far_in, 1),
+        ("lat", lat_size, my_lat, far_out, far_in, 2),
+        ("obs", obs_size, my_obs, parts, parts, 3),
+    )
+    def start_sum():
+        for r in range(2):
+            near_out[:, :, r * share : (r + 1) * share, :] = (
+                total[r].reshape(obs_size, lat_size, share, width).astype(BF16)
+            )
+        near_in[my_obs] = near_out[my_obs]
+        around(*stages[0])
+
     span = 128
 
     def degrees_of(q, carry):
@@ -558,6 +599,7 @@
             return inner
 
         lax.fori_loop(0, degrees // span, degree_tile, 0)
+        pl.when(q == chunks - 1)(start_sum)
         for i in range(CHUNK):
             by_lat[i * lat_count : (i + 1) * lat_count, :] = (
                 dot(leg_ref[q * CHUNK + i], coeff_ref[i]) * quad
@@ -573,43 +615,6 @@
 
     lax.fori_loop(0, chunks, degrees_of, 0)
 
-    share = degrees // group
-
-    def around(axis, size, mine, src, dst, sem):
-        def step(j, carry):
-            peer = lax.rem(mine + j, size)
-            send(
-                src.at[peer],
-                dst.at[mine],
-                sum_send.at[sem],
-                sum_recv.at[sem],
-                {axis: peer},
-            ).start()
-            return carry
-
-        lax.fori_loop(1, size, step, 0)
-
-    def landed(axis, size, mine, src, dst, sem):
-        return send(
-            src.at[pl.ds(0, size - 1)],
-            dst.at[pl.ds(0, size - 1)],
-            sum_send.at[sem],
-            sum_recv.at[sem],
-            {axis: lax.rem(mine + 1, size)},
-        )
-
-    stages = (
-        ("obs", obs_size, my_obs, near_out, near_in, 0),
-        ("lat", lat_size, my_lat, far_out, far_in, 1),
-        ("lat", lat_size, my_lat, far_out, far_in, 2),
-        ("obs", obs_size, my_obs, parts, parts, 3),
-    )
-    for r in range(2):
-        near_out[:, :, r * share : (r + 1) * share, :] = (
-            total[r].reshape(obs_size, lat_size, share, width).astype(BF16)
-        )
-    near_in[my_obs] = near_out[my_obs]
-    around(*stages[0])
     hot_t[...] = jnp.where(iota((orders, orders), 0) == order_row[...], 1.0, 0.0).astype(BF16)
     local[3].wait()
     make_tab_t(0)
@@ -634,13 +639,6 @@
 
     lax.fori_loop(1, lat_size, spread_out, 0)
 
-    send(
-        bwd_out.at[:, pl.ds(0, group - 1)],
-        bwd_in.at[pl.ds(0, group - 1)],
-        bwd_send,
-        bwd_recv,
-        beside,
-    ).wait_recv()
     landed(*stages[2]).wait_recv()
 
     def spread_wide(j, carry):
@@ -655,6 +653,14 @@
 
     lax.fori_loop(1, obs_size, spread_wide, 0)
 
+    send(
+        bwd_out.at[:, pl.ds(0, group - 1)],
+        bwd_in.at[pl.ds(0, group - 1)],
+        bwd_send,
+        bwd_recv,
+        beside,
+    ).wait_recv()
+
     back = bwd_in[...].astype(F32).reshape(group * chunks, lat_dev, CHUNK, 2 * width)
     for part in range(2):
         lane = slice(part * width, (part + 1) * width)
@@ -662,22 +668,29 @@
             [back[:, k, :, lane].reshape(orders, width) for k in range(lat_dev)], axis=1
         ).astype(BF16)
 
-    def to_grid(i, carry):
-        at = pl.multiple_of(i * tile, tile)
-        got = dot(tab_t[pl.ds(at, tile), :], pre_ref[0 : 2 * orders, :]) * (1.0 / lon_count)
+    leaving = []
+    for i in range(lon_count // tile):
+        here = slice(i * tile, (i + 1) * tile)
+        got = dot(tab_t[here, :], pre_ref[0 : 2 * orders, :]) * (1.0 / lon_count)
         for k in range(lat_dev):
-            grid_out[k, pl.ds(at, tile), :] = (
-                out_ref[k, pl.ds(at, tile), :] + got[:, k * width : (k + 1) * width]
+            grid_ref[k, here, :] = (
+                out_ref[k, here, :] + got[:, k * width : (k + 1) * width]
             ).astype(BF16)
-        return carry
-
-    lax.fori_loop(0, lon_count // tile, to_grid, 0)
+        leaving.append(
+            pltpu.make_async_copy(grid_ref.at[:, here], grid_out.at[:, here], leave_sem.at[i])
+        )
+        leaving[-1].start()
 
     landed(*stages[3]).wait_recv()
     for r in range(2):
-        gain_out[r] = (
-            parts[:, :, r * share : (r + 1) * share, :].astype(F32).reshape(degrees, width)
-        )
+        leaving.append(
+            pltpu.make_async_copy(
+                parts.at[:, :, r * share : (r + 1) * share],
+                gain_out.at[r],
+                leave_sem.at[lon_count // tile + r],
+            )
+        )
+        leaving[-1].start()
 
     send(
         packed.at[pl.ds(0, group - 1)], obs_in.at[pl.ds(0, group - 1)], obs_send, obs_recv, beside
@@ -700,6 +713,8 @@
     landed(*stages[1]).wait_send()
     landed(*stages[2]).wait_send()
     landed(*stages[3]).wait_send()
+    for copy in leaving:
+        copy.wait()
 
 
 def on_device(
@@ -735,14 +750,14 @@
     anywhere = pl.BlockSpec(memory_space=pltpu.HBM)
     dma = pltpu.SemaphoreType.DMA
     share = degrees // group
-    return pl.pallas_call(
+    grid_grad, gain_parts = pl.pallas_call(
         functools.partial(block_kernel, lat_size, obs_size),
         out_shape=(
             jax.ShapeDtypeStruct((lat_dev, lon_count, width), BF16),
-            jax.ShapeDtypeStruct((2, degrees, width), F32),
+            jax.ShapeDtypeStruct((2, obs_size, lat_size, share, width), BF16),
         ),
         in_specs=[vmem] * 8 + [anywhere] * 7,
-        out_specs=(vmem, vmem),
+        out_specs=(pl.BlockSpec(memory_space=pl.ANY), pl.BlockSpec(memory_space=pl.ANY)),
         scratch_shapes=[
             pltpu.VMEM((lat_dev, lon_count, width), BF16),
             pltpu.VMEM((lat_dev, lon_count, width), BF16),
@@ -770,6 +785,7 @@
             pltpu.VMEM((side, 2 * width), BF16),
             pltpu.VMEM((chunks, group, rows, 2 * width), BF16),
             pltpu.VMEM((group, chunks, rows, 2 * width), BF16),
+            pltpu.VMEM((lat_dev, lon_count, width), BF16),
             pltpu.VMEM((2, degrees, width), F32),
             pltpu.VMEM((obs_size, lat_size, 2 * share, width), BF16),
             pltpu.VMEM((obs_size, lat_size, 2 * share, width), BF16),
@@ -785,9 +801,10 @@
             dma,
             dma((4,)),
             dma((4,)),
+            dma((lon_count // 256 + 2,)),
         ],
         compiler_params=pltpu.CompilerParams(
-            collective_id=0, has_side_effects=True, vmem_limit_bytes=44 * 1024 * 1024
+            collective_id=0, has_side_effects=True, vmem_limit_bytes=60 * 1024 * 1024
         ),
         name="block_backward",
     )(
@@ -807,6 +824,7 @@
         jnp.asarray(table),
         jnp.asarray(table_t),
     )
+    return grid_grad, gain_parts.astype(F32).reshape(2, degrees, width)
 
 
 def kernel_fits(next_grad, legendre, obs_value, lat_size, obs_size):

time: 65.4 us -> 55.1 us (0.84)
  local copies, waits for them, and re-layouts: 14.6 us -> 1.87 us
  other arithmetic: 0 us -> 1.78 us
  Pallas kernels: 49.6 us -> 50.6 us
    unnamed x30 -> x1, local copies, waits for them, and re-layouts: 14.6 us -> 1.87 us
    reshape x0 -> x1, other arithmetic: none -> 1.78 us  [on_device(): return (grid_grad, gain_parts.astype(F32).reshape(2, degrees, width))]
    pallas_call x1, Pallas kernels: 49.6 us -> 50.6 us  [on_device(): pl.pallas_call(functools.partial(block_kernel, lat_size, obs_size), out_s...]
where the time goes in v4:
time: 55.1 us; the launch traced here: 54.9 us
  Pallas kernels  50.6 us (92%)
  local copies, waits for them, and re-layouts  1.87 us (3%)
  other arithmetic  1.78 us (3%)
  between operations  0.64 us (1%)
    pallas_call x1, Pallas kernels, on_device(): pl.pallas_call(functools.partial(block_kernel, lat_size, obs_size), out_s...  50.6 us
    unnamed x1, local copies, waits for them, and re-layouts  1.87 us
    reshape x1, other arithmetic, on_device(): return (grid_grad, gain_parts.astype(F32).reshape(2, degrees, width))  1.78 us

profile of v4, /device:TPU:0, one launch (start us, length us, event | category | flops | bytes accessed | tf_op | source)
XLA Modules:
  0.0 54.9 jit_solution(16590934952912372970)
XLA Ops:
  0.6 50.6 %block_backward.1 = (bf16[2,1024,128]{2,1,0:T(8,128)(2,1)}, bf16[2,4,4,32,128]{4,3,2,1,0:T(8,128)(2,1)}) custom-call(bf16[1,16,16]{2,1,0:T(8,128)(2,1)} %value_ref.1, bf16[1,16,16]{2,1,0:T(8,128)(2,1)} %lat_frac_ref.1, bf16[1,16,16]{2,1,0:T(8,128)(2,1)} %lon_frac_ref.1, s32[1,16,16]{2,1,0:T(8,128)} %corner_ref.1, s32[1,16,16]{2,1,0:T(8,128)} %channel_ref.1, ...), custom_call_target="tpu_custom_call" | custom-call | tf_op jit(solution)/shard_map/block_backward/pallas_call | solution.py:753
  51.2 1.8 %bitcast_convert_fusion = f32[2,512,128]{2,1,0:T(8,128)} fusion(bf16[2,4,4,32,128]{4,3,2,1,0:T(8,128)(2,1)} %get-tuple-element.5), kind=kLoop, calls=%fused_computation | loop fusion | flops 131072 | bytes 786432 | tf_op jit(solution)/shard_map/reshape | solution.py:827
  53.0 1.9 %copy.18 = bf16[2,1024,128]{2,1,0:T(8,128)(2,1)} copy(bf16[2,1024,128]{2,1,0:T(8,128)(2,1)} %get-tuple-element.8) | data formatting | bytes 1048576

commit v5 on v4

--- a/solution.py
+++ b/solution.py
@@ -225,7 +225,7 @@
     return (grid_grad, gain_grad)
 
 
-CHUNK = 8
+CHUNK = 16
 F32 = jnp.float32
 BF16 = jnp.bfloat16
 MESH = pl.DeviceIdType.MESH
@@ -320,8 +320,8 @@
 
     others = []
     for j in range(1, group):
-        lat_at = lax.rem(my_lat + j // obs_size, lat_size)
-        obs_at = lax.rem(my_obs + j % obs_size, obs_size)
+        lat_at = lax.rem(my_lat + j % lat_size, lat_size)
+        obs_at = lax.rem(my_obs + j // lat_size, obs_size)
         others.append((lat_at * obs_size + obs_at, {"lat": lat_at, "obs": obs_at}))
 
     def peers(body):

time: 55.1 us -> 55.6 us (level)
  no operation moved by 1% of the time
where the time goes in v5:
time: 55.6 us; the launch traced here: 55.4 us
  Pallas kernels  51.1 us (92%)
  local copies, waits for them, and re-layouts  1.87 us (3%)
  other arithmetic  1.78 us (3%)
  between operations  0.64 us (1%)
    pallas_call x1, Pallas kernels, on_device(): pl.pallas_call(functools.partial(block_kernel, lat_size, obs_size), out_s...  51.1 us
    unnamed x1, local copies, waits for them, and re-layouts  1.87 us
    reshape x1, other arithmetic, on_device(): return (grid_grad, gain_parts.astype(F32).reshape(2, degrees, width))  1.78 us

profile of v5, /device:TPU:0, one launch (start us, length us, event | category | flops | bytes accessed | tf_op | source)
XLA Modules:
  0.0 55.4 jit_solution(3328531699113250531)
XLA Ops:
  0.6 51.1 %block_backward.1 = (bf16[2,1024,128]{2,1,0:T(8,128)(2,1)}, bf16[2,4,4,32,128]{4,3,2,1,0:T(8,128)(2,1)}) custom-call(bf16[1,16,16]{2,1,0:T(8,128)(2,1)} %value_ref.1, bf16[1,16,16]{2,1,0:T(8,128)(2,1)} %lat_frac_ref.1, bf16[1,16,16]{2,1,0:T(8,128)(2,1)} %lon_frac_ref.1, s32[1,16,16]{2,1,0:T(8,128)} %corner_ref.1, s32[1,16,16]{2,1,0:T(8,128)} %channel_ref.1, ...), custom_call_target="tpu_custom_call" | custom-call | tf_op jit(solution)/shard_map/block_backward/pallas_call | solution.py:753
  51.7 1.8 %bitcast_convert_fusion = f32[2,512,128]{2,1,0:T(8,128)} fusion(bf16[2,4,4,32,128]{4,3,2,1,0:T(8,128)(2,1)} %get-tuple-element.5), kind=kLoop, calls=%fused_computation | loop fusion | flops 131072 | bytes 786432 | tf_op jit(solution)/shard_map/reshape | solution.py:827
  53.5 1.9 %copy.18 = bf16[2,1024,128]{2,1,0:T(8,128)(2,1)} copy(bf16[2,1024,128]{2,1,0:T(8,128)(2,1)} %get-tuple-element.8) | data formatting | bytes 1048576
